TPU v7x, 128 devices: a whole 4x4x4 slice. The times are simulated.
128 devices in a mesh: buf: 8 (over z, core), lat: 4 (over y), lon: 4 (over x).
Axes of the slice: x: 4, y: 4, z: 4, core: 2. Of those that a mesh axis runs over, the one named last changes fastest.
Arguments:
- slots: bfloat16 [8, 4, 4, 2, 1024, 512], P('buf', 'lat', 'lon'), may hold values from -40 to 40
- plan_rank: int32 [4, 4, 8, 1], P('lat', 'lon'), may hold values from 0 to 7; in each aligned block of 8 rows (0 to 7, 8 to 15, ..., all dimensions but the last counted through in order) at most 4 rows name the same one
- plan_slot: int32 [4, 4, 8], P('lat', 'lon'), may hold values from 0 to 1
- gain: float32 [512], replicated, may hold values from 0.5 to 2
- w_qkv: float32 [512, 1536], replicated, may hold values from -0.25 to 0.25
- w_proj: float32 [512, 512], replicated, may hold values from -0.25 to 0.25
- rel_bias: float32 [16, 64, 64], replicated, may hold values from -320 to 320
- cotangent: float32 [8, 1, 128, 128, 512], P('buf', None, 'lat', 'lon'), may hold values from -6 to 6
Outputs:
- block_out: float32 [8, 1, 128, 128, 512], P('buf', None, 'lat', 'lon')
- grad_qkv: float32 [512, 1536], P(('buf', 'lat', 'lon'))
- grad_proj: float32 [512, 512], P(('buf', 'lat', 'lon'))
- grad_gain: float32 [512], P(('buf', 'lat', 'lon'))
- grad_rel: float32 [1024, 64], P(('buf', 'lat', 'lon'))
Inputs may be any that keep to these rules, and one draw needn't show every extreme that they name: `plan_rank`: among the 8 samples of one tile, no buffer owner is named more than 4 times; in every draw some tile has exactly 4 samples reading one owner.
All inputs are finite; a program needn't handle non-finite values.
Results may differ from a plain program's by a relative error of at most 0.0011.
Values may be sent and summed in bfloat16 or wider, within the bound.
No kernel may reach another device: no remote copies, remote signals or barrier semaphores. Data moves between devices by JAX's collectives and lax.ppermute only.
A program may use at most 128 MiB of HBM per device.

v0:
```python
import functools
import math

import jax
import jax.numpy as jnp
from jax import lax
from jax.experimental import pallas as pl
from jax.experimental.pallas import tpu as pltpu
from jax.sharding import PartitionSpec as P

HEADS = 16
WSIDE = 8
NT = (((1,), (1,)), ((), ()))
NN = (((1,), (0,)), ((), ()))
f32, bf16 = jnp.float32, jnp.bfloat16


def dot(left, right, dims=NN):
    return lax.dot_general(left, right, dims, preferred_element_type=f32)


def halves(value):
    high = value.astype(bf16)
    return high, (value - high.astype(f32)).astype(bf16)


def window_rows(block):
    pieces = [block[u, 8 * w : 8 * w + 8, :] for w in range(4) for u in range(8)]
    return jnp.concatenate(pieces, axis=0)


def upstream_kernel(scale, cot_ref, phi_ref, plo_ref, uhi_ref, ulo_ref, dohi_ref, dolo_ref, dotok_ref):
    upstream = window_rows(cot_ref) * scale
    uhi, ulo = halves(upstream)
    uhi_ref[...] = uhi
    ulo_ref[...] = ulo
    u3 = jnp.concatenate([uhi, uhi, ulo], axis=1)
    for at in range(0, 512, 128):
        phi = phi_ref[at : at + 128, :]
        rows = jnp.concatenate([phi, plo_ref[at : at + 128, :], phi], axis=1)
        hi, lo = halves(dot(rows, u3, NT))
        dohi_ref[at : at + 128, :], dolo_ref[at : at + 128, :] = hi, lo
        dotok_ref[:, 2 * at : 2 * at + 128] = hi.T
        dotok_ref[:, 2 * at + 128 : 2 * at + 256] = lo.T


def swap(value):
    return jnp.concatenate([value[:, 64:], value[:, :64]], axis=1)


def block_diagonal(value, left, right):
    other = swap(value)
    zeros = jnp.zeros((32, 128), bf16)
    for even, odd in ((value, other), (other, value)):
        first = jnp.concatenate([even[0:32] * left, odd[32:64] * right, zeros, zeros], axis=0)
        second = jnp.concatenate([zeros, zeros, even[64:96] * left, odd[96:128] * right], axis=0)
        yield jnp.concatenate([first, second], axis=1)


def gather_diagonal(lane, pair_a, pair_b):
    low = lane < 64
    return jnp.concatenate(
        [
            jnp.where(low, pair_a[:32], swap(pair_b[:32])),
            jnp.where(low, swap(pair_a[32:]), pair_b[32:]),
        ],
        axis=0,
    )


def heads_product(left2, hi, lo, window):
    zeros = jnp.zeros((64, 256), bf16)
    right = jnp.concatenate([hi, lo, hi, zeros] if window == 0 else [hi, lo, zeros, hi], axis=0)
    product = dot(left2, right)
    return [product[:64, :128], product[64:, 128:]]


def fill(source, step, slot, wcat, xt_all):
    pkhi, pklo, kt, vt, rstd_tok, rstd_lane, qt = slot
    here = pl.ds(pl.multiple_of(step * 256, 256), 256)
    kept = {}

    def project(first):
        for at in range(first, first + 512, 128):
            rows = slice(at, at + 128)
            pkhi[rows, :], pklo[rows, :] = halves(dot(wcat[rows, :], kept["twice"]) * kept["rstd"])

    def turned(base, tok):
        for g in range(4):
            rows = slice(base + 128 * g, base + 128 * g + 128)
            high = pkhi[rows, :].T
            tok[g, :, 0:128] = high
            tok[g, :, 128:256] = pklo[rows, :].T
            if base:
                tok[g, :, 256:384] = high

    def begin():
        tile, side, x_all = source
        rows = [tile[step * 8 + 4 + u].astype(f32) for u in range(8)]
        ends = [side[step * 8 + 4 + u].astype(f32) for u in range(8)]
        pieces = []
        for w in range(4):
            for u in range(8):
                if w < 3:
                    pieces.append(rows[u][8 * w + 4 : 8 * w + 12])
                else:
                    pieces.append(jnp.concatenate([rows[u][28:], ends[u]], axis=0))
        tokens16 = jnp.concatenate(pieces, axis=0).astype(bf16)
        x_all[here, :] = tokens16
        xt = tokens16.T.astype(f32)
        xt16 = xt.astype(bf16)
        xt_all[:, here] = xt16
        mean = jnp.sum(xt, axis=0, keepdims=True) * (1.0 / 512)
        centered = xt - mean
        spread = jnp.sum(centered * centered, axis=0, keepdims=True) * (1.0 / 512)
        rstd = lax.rsqrt(spread + 1e-05)
        rstd_lane[...] = rstd * jnp.ones((8, 1), f32)
        rstd_tok[...] = jnp.transpose(jnp.broadcast_to(rstd, (128, 256)))
        kept["rstd"] = rstd
        kept["twice"] = jnp.concatenate([xt16, xt16], axis=0)

    def queries():
        project(0)
        turned(0, qt)

    def keys():
        project(512)
        turned(512, kt)

    def values():
        project(1024)
        turned(1024, vt)

    return [begin, queries, keys, values]


def main_kernel(
    flag_ref, tile_hbm, down_hbm, right_hbm, corner_hbm, chi_hbm, clo_hbm, bias_hbm, uhi_hbm, ulo_hbm, dohi_ref, dolo_ref, dotok_ref,
    own_hbm, other_hbm, ahi_ref, alo_ref, x_hbm,
    pkhi0, pklo0, kt0, vt0, rt0, rl0, qt0, pkhi1, pklo1, kt1, vt1, rt1, rl1, qt1,
    xt_all, ahi_all, alo_all, g_all, rel_acc,
    wcat, bias_ref, uhi_ref, ulo_ref, own_ref, other_ref, tile, side, x_all, in_sem, out_sem,
):
    step = pl.program_id(0)
    slots = ((pkhi0, pklo0, kt0, vt0, rt0, rl0, qt0), (pkhi1, pklo1, kt1, vt1, rt1, rl1, qt1))
    loads = [
        pltpu.make_async_copy(source, target, in_sem.at[n])
        for n, (source, target) in enumerate(
            (
                (tile_hbm, tile.at[:32]),
                (down_hbm, tile.at[32:]),
                (right_hbm, side.at[:32]),
                (corner_hbm, side.at[32:]),
                (chi_hbm, wcat.at[:, :512]),
                (clo_hbm, wcat.at[:, 512:]),
                (bias_hbm, bias_ref),
                (uhi_hbm, uhi_ref),
                (ulo_hbm, ulo_ref),
            )
        )
    ]
    source = (tile, side, x_all)
    lane = lax.broadcasted_iota(jnp.int32, (1, 128), 1)
    left16 = (lane < 64).astype(f32).astype(bf16)
    right16 = (lane >= 64).astype(f32).astype(bf16)
    lane2 = lax.broadcasted_iota(jnp.int32, (1, 256), 1) & 127
    head_of = [((lane2 >= 32 * j) & (lane2 < 32 * j + 32)).astype(f32).astype(bf16) for j in range(4)]
    row_of = lax.broadcasted_iota(jnp.int32, (64, 256), 0)
    lane_of = lax.broadcasted_iota(jnp.int32, (64, 256), 1)
    root = 1.0 / math.sqrt(32.0)

    def operands(g, slot):
        pkhi, pklo, kt, vt = slot[:4]
        rows_q, rows_k, rows_v = (slice(128 * g + base, 128 * g + base + 128) for base in (0, 512, 1024))
        unit = []
        for p in range(2):
            lanes = slice(128 * p, 128 * p + 128)
            qhi = list(block_diagonal(pkhi[rows_q, lanes], left16, right16))
            qlo = list(block_diagonal(pklo[rows_q, lanes], left16, right16))
            ohi = list(block_diagonal(dohi_ref[rows_q, lanes], left16, right16))
            olo = list(block_diagonal(dolo_ref[rows_q, lanes], left16, right16))
            both = []
            for rows in (rows_k, rows_v):
                high, low = pkhi[rows, lanes], pklo[rows, lanes]
                other = swap(high)
                one = high * left16 + other * right16
                two = other * left16 + high * right16
                both.append([jnp.concatenate([one, low], axis=1), jnp.concatenate([two, low], axis=1)])
            for w in range(2):
                unit.append((qhi[w], qlo[w], ohi[w], olo[w], both[0][w], both[1][w]))
        scores, products = [], []
        for n, (qh, ql, oh, ol, _, _) in enumerate(unit):
            at = 64 * n
            scores.append(dot(kt[g, at : at + 64, :], jnp.concatenate([qh, qh, ql], axis=0)))
            products.append(dot(vt[g, at : at + 64, :], jnp.concatenate([oh, oh, ol], axis=0)))
        return unit, scores, products

    def finish(g, state, slot, edge):
        unit, scores, products = state
        rstd_tok, rstd_lane, qt = slot[4:]
        rows_q = slice(128 * g, 128 * g + 128)
        cols_k = slice(128 * g + 512, 128 * g + 640)
        cols_v = slice(128 * g + 1024, 128 * g + 1152)
        probs, attended, dss, grad_q = [], [], [], []
        for n in range(4):
            s = scores[n] + bias_ref[g]
            if edge is not None:
                s = jnp.where(edge, -1000000000.0, s)
            e = jnp.exp(s - jnp.max(s, axis=0, keepdims=True))
            weights = e * (1.0 / jnp.sum(e, axis=0, keepdims=True))
            inner = jnp.sum(weights * products[n], axis=0, keepdims=True)
            probs.append(halves(weights))
            dss.append(weights * (products[n] - inner))
        rel_acc[g] = rel_acc[g] + ((dss[0] + dss[1]) + (dss[2] + dss[3]))
        dss = [halves(ds) for ds in dss]
        for n in range(4):
            attended.append(heads_product(unit[n][5], *probs[n], n % 2))
        for n in range(4):
            grad_q.append(heads_product(unit[n][4], *dss[n], n % 2))
        for pairs, tok, cols in ((probs, None, cols_v), (dss, qt, cols_k)):
            for n in range(4):
                at = 64 * n
                if tok is None:
                    both = dotok_ref[at : at + 64, 256 * g : 256 * g + 256]
                else:
                    both = tok[g, at : at + 64, :]
                to = pl.ds(pl.multiple_of(step * 256 + at, 64), 64)
                to_lo = pl.ds(pl.multiple_of(step * 256 + at + 1024, 64), 64)
                product = dot(
                    jnp.concatenate(pairs[n], axis=0),
                    jnp.concatenate([both * mask for mask in head_of], axis=0),
                )
                total = product[:64, :128] + product[64:, :128] + product[:64, 128:]
                g_all[to, cols], g_all[to_lo, cols] = halves(total * rstd_tok[at : at + 64, :])
        for p in range(2):
            lanes = slice(128 * p, 128 * p + 128)
            here_p = pl.ds(pl.multiple_of(step * 256 + 128 * p, 128), 128)
            here_p_lo = pl.ds(pl.multiple_of(step * 256 + 128 * p + 1024, 128), 128)
            one, two = 2 * p, 2 * p + 1
            att = jnp.concatenate([gather_diagonal(lane, attended[one][t], attended[two][t]) for t in range(2)], axis=0)
            att_hi, att_lo = halves(att)
            ahi_all[rows_q, here_p], alo_all[rows_q, here_p] = att_hi, att_lo
            ahi_ref[rows_q, lanes], alo_ref[rows_q, lanes] = att_hi, att_lo
            gq = jnp.concatenate([gather_diagonal(lane, grad_q[one][t], grad_q[two][t]) for t in range(2)], axis=0)
            gq = gq * (rstd_lane[0:1, lanes] * root)
            gq_hi, gq_lo = halves(gq)
            g_all[here_p, rows_q], g_all[here_p_lo, rows_q] = gq_hi.T, gq_lo.T

    def attention(slot, beside, edge):
        state = operands(0, slot)
        for g in range(4):
            if beside is not None:
                beside[g]()
            after = operands(g + 1, slot) if g < 3 else None
            finish(g, state, slot, edge)
            state = after

    @pl.when(step == 0)
    def _():
        for load in loads:
            load.start()
        rel_acc[...] = jnp.zeros_like(rel_acc)
        parts = fill(source, 0, slots[0], wcat, xt_all)
        for load in loads[:4]:
            load.wait()
        parts[0]()
        loads[4].wait()
        loads[5].wait()
        for part in parts[1:]:
            part()
        loads[6].wait()

    @pl.when(step % 2 == 0)
    def _():
        attention(slots[0], fill(source, step + 1, slots[1], wcat, xt_all), None)

    @pl.when(step == 1)
    def _():
        attention(slots[1], fill(source, step + 1, slots[0], wcat, xt_all), None)

    @pl.when(step == 3)
    def _():
        keep = pltpu.make_async_copy(x_all, x_hbm, in_sem.at[9])
        keep.start()
        crossing = ((row_of >= 32) != ((lane_of & 63) >= 32)) & (flag_ref[0] > 0)
        attention(slots[1], None, crossing)
        loads[7].wait()
        loads[8].wait()
        sub = lax.broadcasted_iota(jnp.int32, (1, 8, 128), 1)
        first = flag_ref[1] == 0
        stores = [keep]

        def send(k):
            for n, (source, target) in enumerate(((own_ref, own_hbm), (other_ref, other_hbm))):
                copy = pltpu.make_async_copy(
                    source.at[k], target.at[k], out_sem.at[n, k]
                )
                copy.start()
                stores.append(copy)

        def pack(k, value):
            a, b = value[:, :128].reshape(64, 8, 128), value[:, 128:].reshape(64, 8, 128)
            aa = jnp.concatenate([a[:, 4:], a[:, :4]], axis=1)
            bb = jnp.concatenate([b[:, 4:], b[:, :4]], axis=1)
            even = jnp.where(sub < 4, a, bb).reshape(4, 2, 8, 8, 128)
            odd = jnp.where(sub < 4, aa, b).reshape(4, 2, 8, 8, 128)
            for n, block in ((0, even), (1, odd)):
                own_ref[k, :, :, n] = jnp.where(first, block[:, 0], block[:, 1])
                other_ref[k, :, :, n] = jnp.where(first, block[:, 1], block[:, 0])
            send(k)

        twice = jnp.concatenate([xt_all[...], xt_all[...]], axis=1)
        for k in range(6):
            value = dot(twice, g_all[:, 256 * k : 256 * k + 256])
            pack(k, value - jnp.sum(value, axis=0, keepdims=True) * (1.0 / 512))
        for k in range(2):
            cols = slice(256 * k, 256 * k + 256)
            u = uhi_ref[:, cols]
            value = (
                dot(ahi_all[...], u) + dot(alo_all[...], u) + dot(ahi_all[...], ulo_ref[:, cols])
            )
            pack(6 + k, value)
        for g in range(4):
            turned = jnp.transpose(
                jnp.concatenate([rel_acc[g], jnp.zeros((64, 256), f32)], axis=0)
            ).reshape(2, 8, 2, 8, 128)
            own_ref[8, g] = jnp.where(first, turned[0], turned[1])
            other_ref[8, g] = jnp.where(first, turned[1], turned[0])
        send(8)
        for store in stores:
            store.wait()


def output_kernel(x_ref, ahi_ref, alo_ref, phi_ref, plo_ref, out_ref):
    tokens = x_ref[...].astype(f32)
    tok_hi, tok_lo = ahi_ref[...].T, alo_ref[...].T
    phi = phi_ref[...]
    wp3 = jnp.concatenate([phi, phi, plo_ref[...]], axis=0)
    result = tokens + dot(jnp.concatenate([tok_hi, tok_lo, tok_hi], axis=1), wp3)
    for w in range(4):
        for u in range(8):
            out_ref[u, 8 * w : 8 * w + 8, :] = result[64 * w + 8 * u : 64 * w + 8 * u + 8, :]


def full(shape):
    return pl.BlockSpec(shape, lambda a: (0,) * len(shape))


def once(shape):
    return pl.BlockSpec(shape, lambda a: (0,) * len(shape), pipeline_mode=pl.Buffered(1))


def upstream_call(cot, phi, plo, scale):
    return pl.pallas_call(
        functools.partial(upstream_kernel, scale),
        grid=(4,),
        in_specs=[pl.BlockSpec((8, 32, 512), lambda a: (a, 0, 0))] + [full((512, 512))] * 2,
        out_specs=[
            pl.BlockSpec((256, 512), lambda a: (a, 0)),
            pl.BlockSpec((256, 512), lambda a: (a, 0)),
            pl.BlockSpec((512, 256), lambda a: (0, a)),
            pl.BlockSpec((512, 256), lambda a: (0, a)),
            pl.BlockSpec((256, 1024), lambda a: (a, 0)),
        ],
        out_shape=[jax.ShapeDtypeStruct((1024, 512), bf16)] * 2
        + [jax.ShapeDtypeStruct((512, 1024), bf16)] * 2
        + [jax.ShapeDtypeStruct((1024, 1024), bf16)],
        compiler_params=pltpu.CompilerParams(vmem_limit_bytes=24 << 20),
        cost_estimate=pl.CostEstimate(flops=1600000000, bytes_accessed=8 << 20, transcendentals=0),
        name="upstream",
    )(cot, phi, plo)


def main_call(flags, tile, down, right, corner, chi, clo, bias, uhi, ulo, dohi, dolo, dotok):
    anywhere = pl.BlockSpec(memory_space=pl.ANY)
    column = pl.BlockSpec((512, 256), lambda a: (0, a))
    slot = [
        pltpu.VMEM((1536, 256), bf16),
        pltpu.VMEM((1536, 256), bf16),
        pltpu.VMEM((4, 256, 384), bf16),
        pltpu.VMEM((4, 256, 384), bf16),
        pltpu.VMEM((256, 128), f32),
        pltpu.VMEM((8, 256), f32),
        pltpu.VMEM((4, 256, 256), bf16),
    ]
    terms = (9, 4, 8, 2, 8, 128)
    return pl.pallas_call(
        main_kernel,
        grid=(4,),
        in_specs=[pl.BlockSpec(memory_space=pltpu.SMEM)]
        + [anywhere] * 9
        + [column] * 2
        + [pl.BlockSpec((256, 1024), lambda a: (a, 0))],
        out_specs=[anywhere] * 2 + [column] * 2 + [anywhere],
        out_shape=[jax.ShapeDtypeStruct(terms, f32)] * 2
        + [jax.ShapeDtypeStruct((512, 1024), bf16)] * 2
        + [jax.ShapeDtypeStruct((1024, 512), bf16)],
        scratch_shapes=slot
        + slot
        + [
            pltpu.VMEM((512, 1024), bf16),
            pltpu.VMEM((512, 1024), bf16),
            pltpu.VMEM((512, 1024), bf16),
            pltpu.VMEM((2048, 1536), bf16),
            pltpu.VMEM((4, 64, 256), f32),
            pltpu.VMEM((1536, 1024), bf16),
            pltpu.VMEM((4, 64, 256), f32),
            pltpu.VMEM((1024, 512), bf16),
            pltpu.VMEM((1024, 512), bf16),
            pltpu.VMEM(terms, f32),
            pltpu.VMEM(terms, f32),
            pltpu.VMEM((36, 32, 512), bf16),
            pltpu.VMEM((36, 4, 512), bf16),
            pltpu.VMEM((1024, 512), bf16),
            pltpu.SemaphoreType.DMA((10,)),
            pltpu.SemaphoreType.DMA((2, 9)),
        ],
        compiler_params=pltpu.CompilerParams(vmem_limit_bytes=56 << 20),
        cost_estimate=pl.CostEstimate(flops=16000000000, bytes_accessed=24 << 20, transcendentals=1 << 20),
        name="block",
    )(flags, tile, down, right, corner, chi, clo, bias, uhi, ulo, dohi, dolo, dotok)


def output_call(half, before, x, ahi, alo, phi, plo):
    body, first, given, alias = output_kernel, [], [], {}
    if before is not None:
        first, given, alias = [pl.BlockSpec(memory_space=pl.ANY)], [before], {0: 0}

        def body(_, *refs):
            output_kernel(*refs)

    column = pl.BlockSpec((512, 256), lambda a: (0, a + 2 * half))
    return pl.pallas_call(
        body,
        grid=(2,),
        in_specs=first
        + [pl.BlockSpec((256, 512), lambda a: (a + 2 * half, 0)), column, column] + [once((512, 512))] * 2,
        out_specs=pl.BlockSpec((8, 32, 512), lambda a: (a + 2 * half, 0, 0)),
        out_shape=jax.ShapeDtypeStruct((32, 32, 512), f32),
        input_output_aliases=alias,
        compiler_params=pltpu.CompilerParams(vmem_limit_bytes=56 << 20),
        cost_estimate=pl.CostEstimate(flops=800000000, bytes_accessed=5 << 20, transcendentals=0),
        name="output",
    )(*given, x, ahi, alo, phi, plo)


def split(w):
    high = lax.reduce_precision(w, 8, 7)
    return high.astype(bf16), (w - high).astype(bf16)


def weights(gain, w_qkv, w_proj, rel_bias):
    root = 1.0 / math.sqrt(32.0)
    width = w_proj.shape[0]
    wc = gain[:, None] * w_qkv
    wc = wc * jnp.where(jnp.arange(3 * width) < width, root, 1.0)[None, :]
    wc = (wc - jnp.mean(wc, axis=0, keepdims=True)).T
    bias = rel_bias.reshape(4, 4, 64, 64).transpose(0, 3, 1, 2).reshape(4, 64, 256)
    return split(wc), split(w_proj), bias


ORDER = (0, 2, 1, 3)


def band_kernel(a_ref, b_ref, c_ref, d_ref, gain_ref, rows_ref, qkv_ref, proj_ref, gain_out, rel_ref):
    total = (a_ref[...] + b_ref[...]) + (c_ref[...] + d_ref[...])
    gain = gain_ref[...]
    sums = jnp.zeros((4, 128), f32)
    for k in range(12):
        part = total[4 * k : 4 * k + 4]
        cols = slice(128 * k, 128 * k + 128)
        qkv_ref[:, cols] = part * gain
        sums = sums + part * rows_ref[:, cols]
    for k in range(4):
        proj_ref[:, 128 * k : 128 * k + 128] = total[48 + 4 * k : 52 + 4 * k]
    rel_ref[...] = total[64:, :64]
    column = jnp.sum(sums, axis=1, keepdims=True)
    for n in range(4):
        gain_out[n] = column[n, 0]


def band_call(parts, gain, rows):
    return pl.pallas_call(
        band_kernel,
        out_shape=[
            jax.ShapeDtypeStruct((4, 1536), f32),
            jax.ShapeDtypeStruct((4, 512), f32),
            jax.ShapeDtypeStruct((4,), f32),
            jax.ShapeDtypeStruct((8, 64), f32),
        ],
        out_specs=[pl.BlockSpec(memory_space=pltpu.VMEM)] * 2
        + [pl.BlockSpec(memory_space=pltpu.SMEM), pl.BlockSpec(memory_space=pltpu.VMEM)],
        name="band",
    )(*parts, gain, rows)


def turn(size, by):
    return [(i, (i + by) % size) for i in range(size)]


def fetch(slots, plan_rank, plan_slot, early):
    count = lax.axis_size("buf")
    slot_count, tile_tokens, width = slots.shape[3:]
    part = tile_tokens // count
    spread = slots.reshape(slot_count, count, part, width).transpose(1, 0, 2, 3)
    held = lax.all_to_all(spread, "buf", split_axis=0, concat_axis=0, tiled=True)
    held, early = lax.optimization_barrier((held, early))
    held = held.reshape(count * slot_count, part, width)
    wanted = plan_rank.reshape(count) * slot_count + plan_slot.reshape(count)
    asked = held.at[wanted].get(mode="promise_in_bounds")
    tile = lax.all_to_all(asked, "buf", split_axis=0, concat_axis=0, tiled=True)
    return tile.reshape(32, 32, width), early


def edge_kernel(top_ref, side_ref, down_ref, right_ref, corner_ref):
    half = WSIDE // 2
    down_ref[...] = top_ref[...]
    right_ref[...] = side_ref[:, :half, :]
    corner_ref[...] = top_ref[:, :half, :]


def edge_call(tile):
    half, rows, width = WSIDE // 2, tile.shape[0], tile.shape[-1]
    return pl.pallas_call(
        edge_kernel,
        grid=(1,),
        in_specs=[
            pl.BlockSpec((half, rows, width), lambda a: (0, 0, 0)),
            pl.BlockSpec((rows, 16, width), lambda a: (0, 0, 0)),
        ],
        out_specs=[full((half, rows, width)), full((rows, half, width)), full((half, half, width))],
        out_shape=[
            jax.ShapeDtypeStruct(shape, bf16)
            for shape in ((half, rows, width), (rows, half, width), (half, half, width))
        ],
        compiler_params=pltpu.CompilerParams(vmem_limit_bytes=56 << 20),
        name="edges",
    )(tile, tile)


def halo(tile):
    lat, lon = lax.axis_size("lat"), lax.axis_size("lon")
    down, right, corner = edge_call(tile)
    down = lax.ppermute(down, "lat", turn(lat, -1))
    right = lax.ppermute(right, "lon", turn(lon, -1))
    corner_pairs = [
        (i * lon + j, (i - 1) % lat * lon + (j - 1) % lon) for i in range(lat) for j in range(lon)
    ]
    corner = lax.ppermute(corner, ("lat", "lon"), corner_pairs)
    return tile, down, right, corner


def send(blocks, axis, size, step):
    moved = [lax.ppermute(b, axis, turn(size, step * by)) for b, by in zip(blocks[1:], ORDER[1:])]
    return [blocks[0], *moved]


def choose(blocks, dim, me):
    return [lax.dynamic_index_in_dim(blocks, (me + by) % 4, dim, keepdims=False) for by in ORDER]


def total(parts):
    return (parts[0] + parts[1]) + (parts[2] + parts[3])


def sum_bands(own, other, work):
    buf, lat, lon = lax.axis_index("buf"), lax.axis_index("lat"), lax.axis_index("lon")
    got = lax.ppermute(other, "buf", [(i, i ^ 1) for i in range(8)])
    got, output = lax.optimization_barrier((got, work(0, None)))
    x = (own + got).reshape(9, 4, 4, 4, 8, 128)
    left = send(choose(x[:5], 3, lon), "lon", 4, 1)
    right = total(send(choose(x[5:], 2, lat), "lat", 4, 1))
    left, output = lax.optimization_barrier((left, work(1, output)))
    left = total(left)
    left = total(send(choose(left, 2, lat), "lat", 4, 1))
    right = total(send(choose(right, 2, lon), "lon", 4, 1))
    x = jnp.concatenate([left, right], axis=0)
    return output, [part.reshape(72, 128) for part in send(choose(x, 1, buf // 2), "buf", 8, 2)]


def on_device(slots, plan_rank, plan_slot, gain, w_qkv, w_proj, rel_bias, cotangent):
    width = gain.shape[0]
    wc, wp, bias = weights(gain, w_qkv, w_proj, rel_bias)
    tokens = 128 * cotangent.shape[1] * cotangent.shape[2] * cotangent.shape[3]
    ready = upstream_call(cotangent[0, 0], *wp, 1.0 / math.sqrt(tokens))
    place = (lax.axis_index("buf") * 4 + lax.axis_index("lat")) * 4 + lax.axis_index("lon")
    my_gain = jnp.broadcast_to(lax.dynamic_slice_in_dim(gain, place * 4, 4)[:, None], (4, 128))
    my_rows = lax.dynamic_slice_in_dim(w_qkv, place * 4, 4)
    last = lax.axis_index("lat") == lax.axis_size("lat") - 1
    flags = jnp.stack([last.astype(jnp.int32), lax.axis_index("buf") % 2])
    early = (ready, bias, wp, wc, my_gain, my_rows, flags)
    tile, early = fetch(slots, plan_rank, plan_slot, early)
    ready, bias, wp, wc, my_gain, my_rows, flags = early
    own, other, ahi, alo, x = main_call(flags, *halo(tile), *wc, bias, *ready)
    output, parts = sum_bands(own, other, lambda half, before: output_call(half, before, x, ahi, alo, *wp))
    grad_qkv, grad_proj, grad_gain, grad_rel = band_call(parts, my_gain, my_rows)
    return (output.reshape(cotangent.shape), grad_qkv, grad_proj, grad_gain, grad_rel)


def solution(mesh):
    placed = (
        P("buf", "lat", "lon", None, None, None),
        P("lat", "lon", None, None),
        P("lat", "lon", None),
        P(),
        P(),
        P(),
        P(),
        P("buf", None, "lat", "lon", None),
    )
    return jax.shard_map(
        on_device,
        mesh=mesh,
        in_specs=placed,
        out_specs=(
            P("buf", None, "lat", "lon", None),
            P(("buf", "lat", "lon"), None),
            P(("buf", "lat", "lon"), None),
            P(("buf", "lat", "lon")),
            P(("buf", "lat", "lon"), None),
        ),
        check_vma=False,
    )
```

profile of v0, /device:TPU:0, one launch (start us, length us, event | category | flops | bytes accessed | tf_op | source)
XLA Modules:
  0.0 149.8 jit_solution(15840765995457503612)
XLA Ops:
  0.6 3.1 %copy.37 = bf16[8,2,128,512]{3,2,1,0:T(8,128)(2,1)} copy(bf16[8,2,128,512]{3,2,0,1:T(8,128)(2,1)} %bitcast.97) | data formatting | bytes 4194304 | tf_op jit(solution)/shard_map/transpose | solution.py:505
  3.7 5.7 %all-to-all-start = ((bf16[8,2,128,512]{3,2,1,0:T(8,128)(2,1)}), bf16[8,2,128,512]{3,2,1,0:T(8,128)(2,1)}, u32[]{:S(2)}, u32[]{:S(2)}) async-start(bf16[8,2,128,512]{3,2,1,0:T(8,128)(2,1)} %copy.37), calls=%async_computation | async-start | bytes 4194304 | tf_op jit(solution)/shard_map/all_to_all | solution.py:506
  10.1 2.3 %copy.39 = f32[512,1536]{0,1:T(8,128)} copy(f32[512,1536]{1,0:T(8,128)S(1)} %copy-done.9) | data formatting | bytes 6291456 | tf_op args[4]
  12.4 1.4 copy.38
  16.4 5.4 %upstream.1 = (bf16[1024,512]{1,0:T(8,128)(2,1)S(1)}, bf16[1024,512]{1,0:T(8,128)(2,1)S(1)}, bf16[512,1024]{1,0:T(8,128)(2,1)S(1)}, bf16[512,1024]{1,0:T(8,128)(2,1)S(1)}, bf16[1024,1024]{1,0:T(8,128)(2,1)S(1)}) custom-call(f32[32,32,512]{2,1,0:T(8,128)S(1)} %bitcast.89, bf16[512,512]{1,0:T(8,128)(2,1)S(1)} %get-tuple-element.66.phi_ref.refs_3_, ...), custom_call_target="tpu_custom_call" | custom-call | flops 1600000000 | bytes 8388608 | tf_op jit(solution)/shard_map/upstream/pallas_call | solution.py:354
  26.4 1.4 constant_dynamic-slice_fusion.rows_ref
  27.8 2.1 %fusion = (bf16[1536,512]{1,0:T(8,128)(2,1)}, bf16[1536,512]{1,0:T(8,128)(2,1)}) fusion(f32[512,1536]{0,1:T(8,128)S(1)} %copy-done.8, f32[1536]{0:T(1024)S(1)} %broadcast_multiply_fusion, f32[1536]{0:T(1024)S(1)} %fusion.14, f32[512]{0:T(512)S(1)} %copy-done.15), kind=kLoop, calls=%fused_computation.3 | loop fusion | flops 5505024 | bytes 6305792 | tf_op jit(solution)/shard_map/convert_element_type | solution.py:449
  30.0 6.7 %all-to-all-done = bf16[8,2,128,512]{3,2,1,0:T(8,128)(2,1)} async-done(((bf16[8,2,128,512]{3,2,1,0:T(8,128)(2,1)}), bf16[8,2,128,512]{3,2,1,0:T(8,128)(2,1)}, u32[]{:S(2)}, u32[]{:S(2)}) %all-to-all-start) | async-done | bytes 2097184 | tf_op jit(solution)/shard_map/all_to_all | solution.py:506
  37.3 2.2 %gather_fusion = bf16[8,128,512]{2,1,0:T(8,128)(2,1)S(1)} fusion(bf16[16,128,512]{2,1,0:T(8,128)(2,1)} %bitcast.8, s32[1024]{0:T(1024)S(1)} %pad_clamp_fusion), kind=kCustom, calls=%fused_computation | custom fusion | bytes 2097184 | tf_op jit(solution)/shard_map/gather | solution.py:510
  39.6 19.2 %all_to_all.10 = bf16[8,128,512]{2,1,0:T(8,128)(2,1)} all-to-all(bf16[8,128,512]{2,1,0:T(8,128)(2,1)S(1)} %gather_fusion), channel_id=1, replica_groups=mesh['buf'=8,'lat'=4,'lon'=4] {'buf'}, dimensions={0} | all-to-all | bytes 2097152 | tf_op jit(solution)/shard_map/all_to_all | solution.py:511
  58.8 1.8 %edges.1 = (bf16[4,32,512]{2,1,0:T(8,128)(2,1)}, bf16[32,4,512]{2,1,0:T(4,128)(2,1)}, bf16[4,4,512]{2,1,0:T(4,128)(2,1)}) custom-call(bf16[32,32,512]{2,1,0:T(8,128)(2,1)} %bitcast.90, bf16[32,32,512]{2,1,0:T(8,128)(2,1)} %bitcast.91), custom_call_target="tpu_custom_call" | custom-call | tf_op jit(solution)/shard_map/edges/pallas_call | solution.py:524
  60.6 3.0 %collective-permute-start = (bf16[4,32,512]{2,1,0:T(8,128)(2,1)}, bf16[4,32,512]{2,1,0:T(8,128)(2,1)S(1)}, u32[]{:S(2)}, u32[]{:S(2)}) collective-permute-start(bf16[4,32,512]{2,1,0:T(8,128)(2,1)} %get-tuple-element.50), channel_id=1, source_target_pairs={{0,12},{4,0},{8,4},{12,8},{1,13},{5,1},{9,5},{13,9},{2,14},{6,2},{... | collective-permute-start | bytes 393224 | tf_op jit(solution)/shard_map/ppermute | solution.py:544
  63.6 2.8 %collective-permute-start.1 = (bf16[32,4,512]{2,1,0:T(4,128)(2,1)}, bf16[32,4,512]{2,1,0:T(4,128)(2,1)S(1)}, u32[]{:S(2)}, u32[]{:S(2)}) collective-permute-start(bf16[32,4,512]{2,1,0:T(4,128)(2,1)} %get-tuple-element.51), channel_id=1, source_target_pairs={{0,3},{1,0},{2,1},{3,2},{4,7},{5,4},{6,5},{7,6},{8,11},{9,8},{10,9... | collective-permute-start | bytes 393224 | tf_op jit(solution)/shard_map/ppermute | solution.py:545
  67.4 3.8 %collective-permute-done.2.corner_hbm = bf16[4,4,512]{2,1,0:T(4,128)(2,1)S(1)} collective-permute-done((bf16[4,4,512]{2,1,0:T(4,128)(2,1)}, bf16[4,4,512]{2,1,0:T(4,128)(2,1)S(1)}, u32[]{:S(2)}, u32[]{:S(2)}) %collective-permute-start.2) | collective-permute-done | bytes 16416 | tf_op jit(solution)/shard_map/ppermute | solution.py:549
  72.6 28.4 %block.1 = (f32[9,4,8,2,8,128]{5,4,3,2,1,0:T(8,128)}, f32[9,4,8,2,8,128]{5,4,3,2,1,0:T(8,128)}, bf16[512,1024]{1,0:T(8,128)(2,1)}, bf16[512,1024]{1,0:T(8,128)(2,1)}, bf16[1024,512]{1,0:T(8,128)(2,1)}) custom-call(s32[2]{0:T(128)} %pad_add_fusion.flag_ref, bf16[32,32,512]{2,1,0:T(8,128)(2,1)} %bitcast.92, bf16[4,32,512]{2,1,0:T(8,128)(2,1)} %copy-done.16, ...), custom_call_target="tpu_custom_call" | custom-call | flops 16000000000 | bytes 25165824 | tf_op jit(solution)/shard_map/block/pallas_call | solution.py:387
  101.1 3.7 %output.2._ = f32[32,32,512]{2,1,0:T(8,128)} custom-call(bf16[1024,512]{1,0:T(8,128)(2,1)} %get-tuple-element.63.x_ref.refs_0_, bf16[512,1024]{1,0:T(8,128)(2,1)} %get-tuple-element.64.ahi_ref.refs_1_, bf16[512,1024]{1,0:T(8,128)(2,1)} %get-tuple-element.65.alo_ref.refs_2_, bf16[512,512]{1,0:T(8,128)(2,1)} %copy-done.1, bf16[512,512]{1,0:T(8,128)(2,1)} %copy-done), custom_call_target="tpu_custom_call" | custom-call | flops 800000000 | bytes 5242880 | tf_op jit(solution)/shard_map/output/pallas_call | solution.py:433
  105.8 1.4 copy-done.11
  107.3 2.0 %add.206 = f32[9,4,8,2,8,128]{5,4,3,2,1,0:T(8,128)S(1)} add(f32[9,4,8,2,8,128]{5,4,3,2,1,0:T(8,128)S(1)} %copy-done.10, f32[9,4,8,2,8,128]{5,4,3,2,1,0:T(8,128)} %copy-done.11) | non-fusion elementwise | flops 589824 | bytes 7077888 | tf_op jit(solution)/shard_map/add | solution.py:570
  110.9 2.2 %collective-permute-start.11 = (f32[4,4,4,8,128]{4,3,2,1,0:T(8,128)}, f32[4,4,4,8,128]{4,3,2,1,0:T(8,128)}, u32[]{:S(2)}, u32[]{:S(2)}) collective-permute-start(f32[4,4,4,8,128]{4,3,2,1,0:T(8,128)} %get-tuple-element.88), channel_id=1, source_target_pairs={{0,4},{4,8},{8,12},{12,0},{1,5},{5,9},{9,13},{13,1},{2,6},{6,10},{... | collective-permute-start | bytes 786440 | tf_op jit(solution)/shard_map/ppermute | solution.py:554
  114.5 1.9 %collective-permute-start.4 = (f32[5,4,4,8,128]{4,3,2,1,0:T(8,128)S(1)}, f32[5,4,4,8,128]{4,3,2,1,0:T(8,128)S(1)}, u32[]{:S(2)}, u32[]{:S(2)}) collective-permute-start(f32[5,4,4,8,128]{4,3,2,1,0:T(8,128)S(1)} %get-tuple-element.85), channel_id=1, source_target_pairs={{0,2},{1,3},{2,0},{3,1},{4,6},{5,7},{6,4},{7,5},{8,10},{9,11},{10,... | collective-permute-start | bytes 983048 | tf_op jit(solution)/shard_map/ppermute | solution.py:554
  116.3 1.8 %collective-permute-start.5 = (f32[5,4,4,8,128]{4,3,2,1,0:T(8,128)S(1)}, f32[5,4,4,8,128]{4,3,2,1,0:T(8,128)S(1)}, u32[]{:S(2)}, u32[]{:S(2)}) collective-permute-start(f32[5,4,4,8,128]{4,3,2,1,0:T(8,128)S(1)} %get-tuple-element.84), channel_id=1, source_target_pairs={{0,1},{1,2},{2,3},{3,0},{4,5},{5,6},{6,7},{7,4},{8,9},{9,10},{10,1... | collective-permute-start | bytes 983048 | tf_op jit(solution)/shard_map/ppermute | solution.py:554
  118.2 3.6 %output.3 = f32[32,32,512]{2,1,0:T(8,128)} custom-call(f32[32,32,512]{2,1,0:T(8,128)} %output.2._, bf16[1024,512]{1,0:T(8,128)(2,1)} %get-tuple-element.63.x_ref.refs_0_, bf16[512,1024]{1,0:T(8,128)(2,1)} %get-tuple-element.64.ahi_ref.refs_1_, bf16[512,1024]{1,0:T(8,128)(2,1)} %get-tuple-element.65.alo_ref.refs_2_, ...), custom_call_target="tpu_custom_call", output_to_operand_aliasing={{}: (0, {})} | custom-call | flops 800000000 | bytes 5242880 | tf_op jit(solution)/shard_map/output/pallas_call | solution.py:433
  121.7 1.6 %collective-permute-start.6 = (f32[5,4,4,8,128]{4,3,2,1,0:T(8,128)S(1)}, f32[5,4,4,8,128]{4,3,2,1,0:T(8,128)S(1)}, u32[]{:S(2)}, u32[]{:S(2)}) collective-permute-start(f32[5,4,4,8,128]{4,3,2,1,0:T(8,128)S(1)} %get-tuple-element.83), channel_id=1, source_target_pairs={{0,3},{1,0},{2,1},{3,2},{4,7},{5,4},{6,5},{7,6},{8,11},{9,8},{10,9... | collective-permute-start | bytes 983048 | tf_op jit(solution)/shard_map/ppermute | solution.py:554
  123.4 2.7 %collective-permute-done.11 = f32[4,4,4,8,128]{4,3,2,1,0:T(8,128)} collective-permute-done((f32[4,4,4,8,128]{4,3,2,1,0:T(8,128)}, f32[4,4,4,8,128]{4,3,2,1,0:T(8,128)}, u32[]{:S(2)}, u32[]{:S(2)}) %collective-permute-start.11) | collective-permute-done | bytes 262176 | tf_op jit(solution)/shard_map/ppermute | solution.py:554
  128.2 2.1 %collective-permute-start.14 = (f32[4,4,8,128]{3,2,1,0:T(8,128)S(1)}, f32[4,4,8,128]{3,2,1,0:T(8,128)S(1)}, u32[]{:S(2)}, u32[]{:S(2)}) collective-permute-start(f32[4,4,8,128]{3,2,1,0:T(8,128)S(1)} %get-tuple-element.96), channel_id=1, source_target_pairs={{0,1},{1,2},{2,3},{3,0},{4,5},{5,6},{6,7},{7,4},{8,9},{9,10},{10,1... | collective-permute-start | bytes 196616 | tf_op jit(solution)/shard_map/ppermute | solution.py:554
  133.3 1.4 collective-permute-start.7
  135.2 2.8 %collective-permute-start.9 = (f32[5,4,8,128]{3,2,1,0:T(8,128)S(1)}, f32[5,4,8,128]{3,2,1,0:T(8,128)S(1)}, u32[]{:S(2)}, u32[]{:S(2)}) collective-permute-start(f32[5,4,8,128]{3,2,1,0:T(8,128)S(1)} %get-tuple-element.92), channel_id=1, source_target_pairs={{0,12},{4,0},{8,4},{12,8},{1,13},{5,1},{9,5},{13,9},{2,14},{6,2},{... | collective-permute-start | bytes 245768 | tf_op jit(solution)/shard_map/ppermute | solution.py:554
  138.0 2.2 %collective-permute-done.7 = f32[5,4,8,128]{3,2,1,0:T(8,128)S(1)} collective-permute-done((f32[5,4,8,128]{3,2,1,0:T(8,128)S(1)}, f32[5,4,8,128]{3,2,1,0:T(8,128)S(1)}, u32[]{:S(2)}, u32[]{:S(2)}) %collective-permute-start.7) | collective-permute-done | bytes 81952 | tf_op jit(solution)/shard_map/ppermute | solution.py:554
  141.9 1.6 %collective-permute-start.17 = (f32[9,8,128]{2,1,0:T(8,128)S(1)}, f32[9,8,128]{2,1,0:T(8,128)S(1)}, u32[]{:S(2)}, u32[]{:S(2)}) collective-permute-start(f32[9,8,128]{2,1,0:T(8,128)S(1)} %get-tuple-element.101), channel_id=1, source_target_pairs={{0,32},{16,48},{32,64},{48,80},{64,96},{80,112},{96,0},{112,16},{1... | collective-permute-start | bytes 110600 | tf_op jit(solution)/shard_map/ppermute | solution.py:554
  143.5 1.6 %collective-permute-start.18 = (f32[9,8,128]{2,1,0:T(8,128)S(1)}, f32[9,8,128]{2,1,0:T(8,128)S(1)}, u32[]{:S(2)}, u32[]{:S(2)}) collective-permute-start(f32[9,8,128]{2,1,0:T(8,128)S(1)} %get-tuple-element.98), channel_id=1, source_target_pairs={{0,96},{16,112},{32,0},{48,16},{64,32},{80,48},{96,64},{112,80},{1... | collective-permute-start | bytes 110600 | tf_op jit(solution)/shard_map/ppermute | solution.py:554
  145.1 1.8 %collective-permute-done.16 = f32[9,8,128]{2,1,0:T(8,128)S(1)} collective-permute-done((f32[9,8,128]{2,1,0:T(8,128)S(1)}, f32[9,8,128]{2,1,0:T(8,128)S(1)}, u32[]{:S(2)}, u32[]{:S(2)}) %collective-permute-start.16) | collective-permute-done | bytes 36896 | tf_op jit(solution)/shard_map/ppermute | solution.py:554
  148.1 1.5 band.1
  (85 shorter events, 23.2 us)
Async XLA Ops:
  3.7 5.7 %copy-start.19 = (s32[1,1,8]{2,1,0:T(1,128)S(1)}, s32[1,1,8]{2,1,0:T(1,128)}, u32[]{:S(2)}) copy-start(s32[1,1,8]{2,1,0:T(1,128)} %param.10) | copy-start | bytes 100
  3.7 5.7 %copy-start.20 = (s32[1,1,8,1]{2,3,1,0:T(1,128)S(1)}, s32[1,1,8,1]{2,3,1,0:T(1,128)}, u32[]{:S(2)}) copy-start(s32[1,1,8,1]{2,3,1,0:T(1,128)} %param.9) | copy-start | bytes 100
  3.7 6.3 %copy-start.9 = (f32[512,1536]{1,0:T(8,128)S(1)}, f32[512,1536]{1,0:T(8,128)}, u32[]{:S(2)}) copy-start(f32[512,1536]{1,0:T(8,128)} %param.12) | copy-start | bytes 9437188
  3.7 33.0 %all-to-all-start = ((bf16[8,2,128,512]{3,2,1,0:T(8,128)(2,1)}), bf16[8,2,128,512]{3,2,1,0:T(8,128)(2,1)}, u32[]{:S(2)}, u32[]{:S(2)}) async-start(bf16[8,2,128,512]{3,2,1,0:T(8,128)(2,1)} %copy.37), calls=%async_computation | async-start | bytes 4194304 | tf_op jit(solution)/shard_map/all_to_all | solution.py:506
  10.1 4.8 %copy-start.15 = (f32[512]{0:T(512)S(1)}, f32[512]{0:T(512)}, u32[]{:S(2)}) copy-start(f32[512]{0:T(512)} %param.11) | copy-start | bytes 6148
  12.4 4.0 %copy-start.2 = (f32[1,1,32,32,512]{4,3,2,1,0:T(8,128)S(1)}, f32[1,1,32,32,512]{4,3,2,1,0:T(8,128)}, u32[]{:S(2)}) copy-start(f32[1,1,32,32,512]{4,3,2,1,0:T(8,128)} %param.15) | copy-start | bytes 6291460
  16.3 5.4 %copy-start = (bf16[512,512]{1,0:T(8,128)(2,1)}, bf16[512,512]{1,0:T(8,128)(2,1)S(1)}, u32[]{:S(2)}) copy-start(bf16[512,512]{1,0:T(8,128)(2,1)S(1)} %get-tuple-element.67.plo_ref.refs_4_) | copy-start | bytes 1572868
  16.3 5.4 %copy-start.1 = (bf16[512,512]{1,0:T(8,128)(2,1)}, bf16[512,512]{1,0:T(8,128)(2,1)S(1)}, u32[]{:S(2)}) copy-start(bf16[512,512]{1,0:T(8,128)(2,1)S(1)} %get-tuple-element.66.phi_ref.refs_3_) | copy-start | bytes 1572868
  16.4 8.3 %copy-start.8 = (f32[512,1536]{0,1:T(8,128)S(1)}, f32[512,1536]{0,1:T(8,128)}, u32[]{:S(2)}) copy-start(f32[512,1536]{0,1:T(8,128)} %copy.39) | copy-start | bytes 9437188
  24.7 1.4 copy-start.3
  24.7 1.7 %copy-start.4 = (bf16[1024,512]{1,0:T(8,128)(2,1)}, bf16[1024,512]{1,0:T(8,128)(2,1)S(1)}, u32[]{:S(2)}) copy-start(bf16[1024,512]{1,0:T(8,128)(2,1)S(1)} %get-tuple-element.56.uhi_hbm) | copy-start | bytes 3145732
  60.6 10.6 %collective-permute-start = (bf16[4,32,512]{2,1,0:T(8,128)(2,1)}, bf16[4,32,512]{2,1,0:T(8,128)(2,1)S(1)}, u32[]{:S(2)}, u32[]{:S(2)}) collective-permute-start(bf16[4,32,512]{2,1,0:T(8,128)(2,1)} %get-tuple-element.50), channel_id=1, source_target_pairs={{0,12},{4,0},{8,4},{12,8},{1,13},{5,1},{9,5},{13,9},{2,14},{6,2},{... | collective-permute-start | bytes 393224 | tf_op jit(solution)/shard_map/ppermute | solution.py:544
  63.6 7.6 %collective-permute-start.1 = (bf16[32,4,512]{2,1,0:T(4,128)(2,1)}, bf16[32,4,512]{2,1,0:T(4,128)(2,1)S(1)}, u32[]{:S(2)}, u32[]{:S(2)}) collective-permute-start(bf16[32,4,512]{2,1,0:T(4,128)(2,1)} %get-tuple-element.51), channel_id=1, source_target_pairs={{0,3},{1,0},{2,1},{3,2},{4,7},{5,4},{6,5},{7,6},{8,11},{9,8},{10,9... | collective-permute-start | bytes 393224 | tf_op jit(solution)/shard_map/ppermute | solution.py:545
  66.4 4.8 %collective-permute-start.2 = (bf16[4,4,512]{2,1,0:T(4,128)(2,1)}, bf16[4,4,512]{2,1,0:T(4,128)(2,1)S(1)}, u32[]{:S(2)}, u32[]{:S(2)}) collective-permute-start(bf16[4,4,512]{2,1,0:T(4,128)(2,1)} %get-tuple-element.52), channel_id=1, source_target_pairs={{0,15},{1,12},{2,13},{3,14},{4,3},{5,0},{6,1},{7,2},{8,7},{9,4},{1... | collective-permute-start | bytes 49160 | tf_op jit(solution)/shard_map/ppermute | solution.py:549
  101.0 4.8 %collective-permute-start.3 = (f32[9,4,8,2,8,128]{5,4,3,2,1,0:T(8,128)}, f32[9,4,8,2,8,128]{5,4,3,2,1,0:T(8,128)S(1)}, u32[]{:S(2)}, u32[]{:S(2)}) collective-permute-start(f32[9,4,8,2,8,128]{5,4,3,2,1,0:T(8,128)} %get-tuple-element.62), channel_id=1, source_target_pairs={{0,16},{16,0},{32,48},{48,32},{64,80},{80,64},{96,112},{112,96},{1... | collective-permute-start | bytes 7077896 | tf_op jit(solution)/shard_map/ppermute | solution.py:568
  101.1 6.1 %copy-start.10 = (f32[9,4,8,2,8,128]{5,4,3,2,1,0:T(8,128)S(1)}, f32[9,4,8,2,8,128]{5,4,3,2,1,0:T(8,128)}, u32[]{:S(2)}) copy-start(f32[9,4,8,2,8,128]{5,4,3,2,1,0:T(8,128)} %get-tuple-element.61) | copy-start | bytes 7077892
  105.8 1.4 copy-start.11
  110.3 11.4 %collective-permute-start.10 = (f32[4,4,4,8,128]{4,3,2,1,0:T(8,128)}, f32[4,4,4,8,128]{4,3,2,1,0:T(8,128)}, u32[]{:S(2)}, u32[]{:S(2)}) collective-permute-start(f32[4,4,4,8,128]{4,3,2,1,0:T(8,128)} %get-tuple-element.89), channel_id=1, source_target_pairs={{0,8},{4,12},{8,0},{12,4},{1,9},{5,13},{9,1},{13,5},{2,10},{6,14},... | collective-permute-start | bytes 786440 | tf_op jit(solution)/shard_map/ppermute | solution.py:554
  110.9 15.1 %collective-permute-start.11 = (f32[4,4,4,8,128]{4,3,2,1,0:T(8,128)}, f32[4,4,4,8,128]{4,3,2,1,0:T(8,128)}, u32[]{:S(2)}, u32[]{:S(2)}) collective-permute-start(f32[4,4,4,8,128]{4,3,2,1,0:T(8,128)} %get-tuple-element.88), channel_id=1, source_target_pairs={{0,4},{4,8},{8,12},{12,0},{1,5},{5,9},{9,13},{13,1},{2,6},{6,10},{... | collective-permute-start | bytes 786440 | tf_op jit(solution)/shard_map/ppermute | solution.py:554
  113.1 13.0 %collective-permute-start.12 = (f32[4,4,4,8,128]{4,3,2,1,0:T(8,128)}, f32[4,4,4,8,128]{4,3,2,1,0:T(8,128)}, u32[]{:S(2)}, u32[]{:S(2)}) collective-permute-start(f32[4,4,4,8,128]{4,3,2,1,0:T(8,128)} %get-tuple-element.87), channel_id=1, source_target_pairs={{0,12},{4,0},{8,4},{12,8},{1,13},{5,1},{9,5},{13,9},{2,14},{6,2},{... | collective-permute-start | bytes 786440 | tf_op jit(solution)/shard_map/ppermute | solution.py:554
  114.5 15.8 %collective-permute-start.4 = (f32[5,4,4,8,128]{4,3,2,1,0:T(8,128)S(1)}, f32[5,4,4,8,128]{4,3,2,1,0:T(8,128)S(1)}, u32[]{:S(2)}, u32[]{:S(2)}) collective-permute-start(f32[5,4,4,8,128]{4,3,2,1,0:T(8,128)S(1)} %get-tuple-element.85), channel_id=1, source_target_pairs={{0,2},{1,3},{2,0},{3,1},{4,6},{5,7},{6,4},{7,5},{8,10},{9,11},{10,... | collective-permute-start | bytes 983048 | tf_op jit(solution)/shard_map/ppermute | solution.py:554
  116.3 16.2 %collective-permute-start.5 = (f32[5,4,4,8,128]{4,3,2,1,0:T(8,128)S(1)}, f32[5,4,4,8,128]{4,3,2,1,0:T(8,128)S(1)}, u32[]{:S(2)}, u32[]{:S(2)}) collective-permute-start(f32[5,4,4,8,128]{4,3,2,1,0:T(8,128)S(1)} %get-tuple-element.84), channel_id=1, source_target_pairs={{0,1},{1,2},{2,3},{3,0},{4,5},{5,6},{6,7},{7,4},{8,9},{9,10},{10,1... | collective-permute-start | bytes 983048 | tf_op jit(solution)/shard_map/ppermute | solution.py:554
  121.7 11.4 %collective-permute-start.6 = (f32[5,4,4,8,128]{4,3,2,1,0:T(8,128)S(1)}, f32[5,4,4,8,128]{4,3,2,1,0:T(8,128)S(1)}, u32[]{:S(2)}, u32[]{:S(2)}) collective-permute-start(f32[5,4,4,8,128]{4,3,2,1,0:T(8,128)S(1)} %get-tuple-element.83), channel_id=1, source_target_pairs={{0,3},{1,0},{2,1},{3,2},{4,7},{5,4},{6,5},{7,6},{8,11},{9,8},{10,9... | collective-permute-start | bytes 983048 | tf_op jit(solution)/shard_map/ppermute | solution.py:554
  127.3 7.9 %collective-permute-start.13 = (f32[4,4,8,128]{3,2,1,0:T(8,128)S(1)}, f32[4,4,8,128]{3,2,1,0:T(8,128)S(1)}, u32[]{:S(2)}, u32[]{:S(2)}) collective-permute-start(f32[4,4,8,128]{3,2,1,0:T(8,128)S(1)} %get-tuple-element.97), channel_id=1, source_target_pairs={{0,2},{1,3},{2,0},{3,1},{4,6},{5,7},{6,4},{7,5},{8,10},{9,11},{10,... | collective-permute-start | bytes 196616 | tf_op jit(solution)/shard_map/ppermute | solution.py:554
  128.2 9.8 %collective-permute-start.14 = (f32[4,4,8,128]{3,2,1,0:T(8,128)S(1)}, f32[4,4,8,128]{3,2,1,0:T(8,128)S(1)}, u32[]{:S(2)}, u32[]{:S(2)}) collective-permute-start(f32[4,4,8,128]{3,2,1,0:T(8,128)S(1)} %get-tuple-element.96), channel_id=1, source_target_pairs={{0,1},{1,2},{2,3},{3,0},{4,5},{5,6},{6,7},{7,4},{8,9},{9,10},{10,1... | collective-permute-start | bytes 196616 | tf_op jit(solution)/shard_map/ppermute | solution.py:554
  130.3 7.7 %collective-permute-start.15 = (f32[4,4,8,128]{3,2,1,0:T(8,128)S(1)}, f32[4,4,8,128]{3,2,1,0:T(8,128)S(1)}, u32[]{:S(2)}, u32[]{:S(2)}) collective-permute-start(f32[4,4,8,128]{3,2,1,0:T(8,128)S(1)} %get-tuple-element.95), channel_id=1, source_target_pairs={{0,3},{1,0},{2,1},{3,2},{4,7},{5,4},{6,5},{7,6},{8,11},{9,8},{10,9... | collective-permute-start | bytes 196616 | tf_op jit(solution)/shard_map/ppermute | solution.py:554
  133.3 6.9 %collective-permute-start.7 = (f32[5,4,8,128]{3,2,1,0:T(8,128)S(1)}, f32[5,4,8,128]{3,2,1,0:T(8,128)S(1)}, u32[]{:S(2)}, u32[]{:S(2)}) collective-permute-start(f32[5,4,8,128]{3,2,1,0:T(8,128)S(1)} %get-tuple-element.94), channel_id=1, source_target_pairs={{0,8},{4,12},{8,0},{12,4},{1,9},{5,13},{9,1},{13,5},{2,10},{6,14},... | collective-permute-start | bytes 245768 | tf_op jit(solution)/shard_map/ppermute | solution.py:554
  134.7 6.1 %collective-permute-start.8 = (f32[5,4,8,128]{3,2,1,0:T(8,128)S(1)}, f32[5,4,8,128]{3,2,1,0:T(8,128)S(1)}, u32[]{:S(2)}, u32[]{:S(2)}) collective-permute-start(f32[5,4,8,128]{3,2,1,0:T(8,128)S(1)} %get-tuple-element.93), channel_id=1, source_target_pairs={{0,4},{4,8},{8,12},{12,0},{1,5},{5,9},{9,13},{13,1},{2,6},{6,10},{... | collective-permute-start | bytes 245768 | tf_op jit(solution)/shard_map/ppermute | solution.py:554
  135.2 5.6 %collective-permute-start.9 = (f32[5,4,8,128]{3,2,1,0:T(8,128)S(1)}, f32[5,4,8,128]{3,2,1,0:T(8,128)S(1)}, u32[]{:S(2)}, u32[]{:S(2)}) collective-permute-start(f32[5,4,8,128]{3,2,1,0:T(8,128)S(1)} %get-tuple-element.92), channel_id=1, source_target_pairs={{0,12},{4,0},{8,4},{12,8},{1,13},{5,1},{9,5},{13,9},{2,14},{6,2},{... | collective-permute-start | bytes 245768 | tf_op jit(solution)/shard_map/ppermute | solution.py:554
  141.5 5.5 %collective-permute-start.16 = (f32[9,8,128]{2,1,0:T(8,128)S(1)}, f32[9,8,128]{2,1,0:T(8,128)S(1)}, u32[]{:S(2)}, u32[]{:S(2)}) collective-permute-start(f32[9,8,128]{2,1,0:T(8,128)S(1)} %get-tuple-element.100), channel_id=1, source_target_pairs={{0,64},{16,80},{32,96},{48,112},{64,0},{80,16},{96,32},{112,48},{1... | collective-permute-start | bytes 110600 | tf_op jit(solution)/shard_map/ppermute | solution.py:554
  141.9 5.4 %collective-permute-start.17 = (f32[9,8,128]{2,1,0:T(8,128)S(1)}, f32[9,8,128]{2,1,0:T(8,128)S(1)}, u32[]{:S(2)}, u32[]{:S(2)}) collective-permute-start(f32[9,8,128]{2,1,0:T(8,128)S(1)} %get-tuple-element.101), channel_id=1, source_target_pairs={{0,32},{16,48},{32,64},{48,80},{64,96},{80,112},{96,0},{112,16},{1... | collective-permute-start | bytes 110600 | tf_op jit(solution)/shard_map/ppermute | solution.py:554
  143.5 4.0 %collective-permute-start.18 = (f32[9,8,128]{2,1,0:T(8,128)S(1)}, f32[9,8,128]{2,1,0:T(8,128)S(1)}, u32[]{:S(2)}, u32[]{:S(2)}) collective-permute-start(f32[9,8,128]{2,1,0:T(8,128)S(1)} %get-tuple-element.98), channel_id=1, source_target_pairs={{0,96},{16,112},{32,0},{48,16},{64,32},{80,48},{96,64},{112,80},{1... | collective-permute-start | bytes 110600 | tf_op jit(solution)/shard_map/ppermute | solution.py:554
  (9 other events, 6.7 us)
where the time goes:
time: 150 us
  Pallas kernels  44.4 us (30%)
  starting transfers between devices  34.2 us (23%)
  waiting for transfers between devices  21.1 us (14%)
  local copies, waits for them, and re-layouts  20.8 us (14%)
  blocking collectives  19.2 us (13%)
  other arithmetic  8.95 us (6%)
    pallas_call x1, Pallas kernels, main_call(): pl.pallas_call(main_kernel, grid=(4,), in_specs=[pl.BlockSpec(memory_spac...  28.4 us
    ppermute x15, starting transfers between devices, send(): lax.ppermute(b, axis, turn(size, step * by))  21.7 us
    all_to_all x1, blocking collectives, fetch(): tile = lax.all_to_all(asked, 'buf', split_axis=0, concat_axis=0, tiled=True)  19.2 us
    unnamed x43, local copies, waits for them, and re-layouts  9.57 us
    ppermute x15, waiting for transfers between devices, send(): lax.ppermute(b, axis, turn(size, step * by))  9.53 us
    pallas_call x2, Pallas kernels, output_call(): pl.pallas_call(body, grid=(2,), in_specs=first + [pl.BlockSpec((256, 512)...  7.28 us
    all_to_all x1, waiting for transfers between devices, fetch(): lax.all_to_all(spread, 'buf', split_axis=0, concat_axis=0, tiled=True)  6.74 us
    all_to_all x1, starting transfers between devices, fetch(): lax.all_to_all(spread, 'buf', split_axis=0, concat_axis=0, tiled=True)  5.66 us
  transfers between devices with their start and end apart: 20, of which 11 were waited for; matrix products, arithmetic and copies ran while one was open for 9% of the time, Pallas kernels for 8%

commit v1 on v0

--- a/solution.py
+++ b/solution.py
@@ -9,6 +9,7 @@
 from jax.sharding import PartitionSpec as P
 
 HEADS = 16
+SPLIT = 5
 WSIDE = 8
 NT = (((1,), (1,)), ((), ()))
 NN = (((1,), (0,)), ((), ()))
@@ -136,7 +137,7 @@
 
 def main_kernel(
     flag_ref, tile_hbm, down_hbm, right_hbm, corner_hbm, chi_hbm, clo_hbm, bias_hbm, uhi_hbm, ulo_hbm, dohi_ref, dolo_ref, dotok_ref,
-    own_hbm, other_hbm, ahi_ref, alo_ref, x_hbm,
+    own_left, own_right, other_left, other_right, ahi_ref, alo_ref, x_hbm,
     pkhi0, pklo0, kt0, vt0, rt0, rl0, qt0, pkhi1, pklo1, kt1, vt1, rt1, rl1, qt1,
     xt_all, ahi_all, alo_all, g_all, rel_acc,
     wcat, bias_ref, uhi_ref, ulo_ref, own_ref, other_ref, tile, side, x_all, in_sem, out_sem,
@@ -291,10 +292,11 @@
         stores = [keep]
 
         def send(k):
-            for n, (source, target) in enumerate(((own_ref, own_hbm), (other_ref, other_hbm))):
-                copy = pltpu.make_async_copy(
-                    source.at[k], target.at[k], out_sem.at[n, k]
-                )
+            for n, (source, left, right) in enumerate(
+                ((own_ref, own_left, own_right), (other_ref, other_left, other_right))
+            ):
+                target = left.at[k] if k < SPLIT else right.at[k - SPLIT]
+                copy = pltpu.make_async_copy(source.at[k], target, out_sem.at[n, k])
                 copy.start()
                 stores.append(copy)
 
@@ -391,8 +393,8 @@
         + [anywhere] * 9
         + [column] * 2
         + [pl.BlockSpec((256, 1024), lambda a: (a, 0))],
-        out_specs=[anywhere] * 2 + [column] * 2 + [anywhere],
-        out_shape=[jax.ShapeDtypeStruct(terms, f32)] * 2
+        out_specs=[anywhere] * 4 + [column] * 2 + [anywhere],
+        out_shape=[jax.ShapeDtypeStruct((n, *terms[1:]), f32) for n in (SPLIT, 9 - SPLIT)] * 2
         + [jax.ShapeDtypeStruct((512, 1024), bf16)] * 2
         + [jax.ShapeDtypeStruct((1024, 512), bf16)],
         scratch_shapes=slot
@@ -563,13 +565,16 @@
     return (parts[0] + parts[1]) + (parts[2] + parts[3])
 
 
-def sum_bands(own, other, work):
+def sum_bands(terms, work):
     buf, lat, lon = lax.axis_index("buf"), lax.axis_index("lat"), lax.axis_index("lon")
-    got = lax.ppermute(other, "buf", [(i, i ^ 1) for i in range(8)])
-    got, output = lax.optimization_barrier((got, work(0, None)))
-    x = (own + got).reshape(9, 4, 4, 4, 8, 128)
-    left = send(choose(x[:5], 3, lon), "lon", 4, 1)
-    right = total(send(choose(x[5:], 2, lat), "lat", 4, 1))
+    own_left, own_right, other_left, other_right = terms
+    pairs = [(i, i ^ 1) for i in range(8)]
+    got_left = lax.ppermute(other_left, "buf", pairs)
+    got_right, output = lax.optimization_barrier((lax.ppermute(other_right, "buf", pairs), work(0, None)))
+    left = (own_left + got_left).reshape(SPLIT, 4, 4, 4, 8, 128)
+    right = (own_right + got_right).reshape(9 - SPLIT, 4, 4, 4, 8, 128)
+    left = send(choose(left, 3, lon), "lon", 4, 1)
+    right = total(send(choose(right, 2, lat), "lat", 4, 1))
     left, output = lax.optimization_barrier((left, work(1, output)))
     left = total(left)
     left = total(send(choose(left, 2, lat), "lat", 4, 1))
@@ -591,8 +596,8 @@
     early = (ready, bias, wp, wc, my_gain, my_rows, flags)
     tile, early = fetch(slots, plan_rank, plan_slot, early)
     ready, bias, wp, wc, my_gain, my_rows, flags = early
-    own, other, ahi, alo, x = main_call(flags, *halo(tile), *wc, bias, *ready)
-    output, parts = sum_bands(own, other, lambda half, before: output_call(half, before, x, ahi, alo, *wp))
+    *terms, ahi, alo, x = main_call(flags, *halo(tile), *wc, bias, *ready)
+    output, parts = sum_bands(terms, lambda half, before: output_call(half, before, x, ahi, alo, *wp))
     grad_qkv, grad_proj, grad_gain, grad_rel = band_call(parts, my_gain, my_rows)
     return (output.reshape(cotangent.shape), grad_qkv, grad_proj, grad_gain, grad_rel)
 

time: 150 us -> 152 us (1.013)
  waiting for transfers between devices: 21.1 us -> 26.1 us
  local copies, waits for them, and re-layouts: 20.8 us -> 18.7 us
  other arithmetic: 8.95 us -> 7.2 us
    ppermute x15, waiting for transfers between devices: 9.53 us -> 14.8 us  [send(): lax.ppermute(b, axis, turn(size, step * by))]
    unnamed x43, local copies, waits for them, and re-layouts: 9.57 us -> 7.77 us
    add x1 -> x2, other arithmetic: 2.01 us -> 0.31 us  [the longest x1 0.17 us: sum_bands(): left = (own_left + got_left).reshape(SPLIT, 4, 4, 4, 8, 128)]
  transfers between devices with their start and end apart: 20 -> 21, of which waited for: 11 -> 13; matrix products, arithmetic and copies ran while one was open for 9% -> 9% of each run, Pallas kernels for 8% -> 8%
where the time goes in v1:
time: 152 us; the launch traced here: 151 us
  Pallas kernels  44.4 us (29%)
  starting transfers between devices  34.5 us (23%)
  waiting for transfers between devices  26.1 us (17%)
  blocking collectives  19.2 us (13%)
  local copies, waits for them, and re-layouts  18.7 us (12%)
  other arithmetic  7.2 us (5%)
    pallas_call x1, Pallas kernels, main_call(): pl.pallas_call(main_kernel, grid=(4,), in_specs=[pl.BlockSpec(memory_spac...  28.4 us
    ppermute x15, starting transfers between devices, send(): lax.ppermute(b, axis, turn(size, step * by))  21.4 us
    all_to_all x1, blocking collectives, fetch(): tile = lax.all_to_all(asked, 'buf', split_axis=0, concat_axis=0, tiled=True)  19.2 us
    ppermute x15, waiting for transfers between devices, send(): lax.ppermute(b, axis, turn(size, step * by))  14.8 us
    unnamed x43, local copies, waits for them, and re-layouts  7.77 us
    pallas_call x2, Pallas kernels, output_call(): pl.pallas_call(body, grid=(2,), in_specs=first + [pl.BlockSpec((256, 512)...  7.3 us
    all_to_all x1, waiting for transfers between devices, fetch(): lax.all_to_all(spread, 'buf', split_axis=0, concat_axis=0, tiled=True)  6.95 us
    all_to_all x1, starting transfers between devices, fetch(): lax.all_to_all(spread, 'buf', split_axis=0, concat_axis=0, tiled=True)  5.66 us
  transfers between devices with their start and end apart: 21, of which 13 were waited for; matrix products, arithmetic and copies ran while one was open for 9% of the time, Pallas kernels for 8%

profile of v1, /device:TPU:0, one launch (start us, length us, event | category | flops | bytes accessed | tf_op | source)
XLA Modules:
  0.0 151.2 jit_solution(15493987916496980886)
XLA Ops:
  0.6 3.1 %copy.37 = bf16[8,2,128,512]{3,2,1,0:T(8,128)(2,1)} copy(bf16[8,2,128,512]{3,2,0,1:T(8,128)(2,1)} %bitcast.97) | data formatting | bytes 4194304 | tf_op jit(solution)/shard_map/transpose | solution.py:507
  3.7 5.7 %all-to-all-start = ((bf16[8,2,128,512]{3,2,1,0:T(8,128)(2,1)}), bf16[8,2,128,512]{3,2,1,0:T(8,128)(2,1)}, u32[]{:S(2)}, u32[]{:S(2)}) async-start(bf16[8,2,128,512]{3,2,1,0:T(8,128)(2,1)} %copy.37), calls=%async_computation | async-start | bytes 4194304 | tf_op jit(solution)/shard_map/all_to_all | solution.py:508
  10.1 2.4 %copy.39 = f32[512,1536]{0,1:T(8,128)} copy(f32[512,1536]{1,0:T(8,128)S(1)} %copy-done.9) | data formatting | bytes 6291456 | tf_op args[4]
  12.4 1.4 copy.38
  16.4 5.4 %upstream.1 = (bf16[1024,512]{1,0:T(8,128)(2,1)S(1)}, bf16[1024,512]{1,0:T(8,128)(2,1)S(1)}, bf16[512,1024]{1,0:T(8,128)(2,1)S(1)}, bf16[512,1024]{1,0:T(8,128)(2,1)S(1)}, bf16[1024,1024]{1,0:T(8,128)(2,1)S(1)}) custom-call(f32[32,32,512]{2,1,0:T(8,128)S(1)} %bitcast.89, bf16[512,512]{1,0:T(8,128)(2,1)S(1)} %get-tuple-element.69.phi_ref.refs_3_, ...), custom_call_target="tpu_custom_call" | custom-call | flops 1600000000 | bytes 8388608 | tf_op jit(solution)/shard_map/upstream/pallas_call | solution.py:356
  26.1 1.4 constant_dynamic-slice_fusion.rows_ref
  27.5 2.2 %fusion = (bf16[1536,512]{1,0:T(8,128)(2,1)}, bf16[1536,512]{1,0:T(8,128)(2,1)}) fusion(f32[512,1536]{0,1:T(8,128)S(1)} %copy-done.8, f32[1536]{0:T(1024)S(1)} %broadcast_multiply_fusion, f32[1536]{0:T(1024)S(1)} %fusion.14, f32[512]{0:T(512)S(1)} %copy-done.15), kind=kLoop, calls=%fused_computation.3 | loop fusion | flops 5505024 | bytes 6305792 | tf_op jit(solution)/shard_map/convert_element_type | solution.py:451
  29.7 7.0 %all-to-all-done = bf16[8,2,128,512]{3,2,1,0:T(8,128)(2,1)} async-done(((bf16[8,2,128,512]{3,2,1,0:T(8,128)(2,1)}), bf16[8,2,128,512]{3,2,1,0:T(8,128)(2,1)}, u32[]{:S(2)}, u32[]{:S(2)}) %all-to-all-start) | async-done | bytes 2097184 | tf_op jit(solution)/shard_map/all_to_all | solution.py:508
  37.4 2.2 %gather_fusion = bf16[8,128,512]{2,1,0:T(8,128)(2,1)S(1)} fusion(bf16[16,128,512]{2,1,0:T(8,128)(2,1)} %bitcast.8, s32[1024]{0:T(1024)S(1)} %pad_clamp_fusion), kind=kCustom, calls=%fused_computation | custom fusion | bytes 2097184 | tf_op jit(solution)/shard_map/gather | solution.py:512
  39.6 19.2 %all_to_all.10 = bf16[8,128,512]{2,1,0:T(8,128)(2,1)} all-to-all(bf16[8,128,512]{2,1,0:T(8,128)(2,1)S(1)} %gather_fusion), channel_id=1, replica_groups=mesh['buf'=8,'lat'=4,'lon'=4] {'buf'}, dimensions={0} | all-to-all | bytes 2097152 | tf_op jit(solution)/shard_map/all_to_all | solution.py:513
  58.8 1.8 %edges.1 = (bf16[4,32,512]{2,1,0:T(8,128)(2,1)}, bf16[32,4,512]{2,1,0:T(4,128)(2,1)}, bf16[4,4,512]{2,1,0:T(4,128)(2,1)}) custom-call(bf16[32,32,512]{2,1,0:T(8,128)(2,1)} %bitcast.90, bf16[32,32,512]{2,1,0:T(8,128)(2,1)} %bitcast.91), custom_call_target="tpu_custom_call" | custom-call | tf_op jit(solution)/shard_map/edges/pallas_call | solution.py:526
  60.6 3.0 %collective-permute-start = (bf16[4,32,512]{2,1,0:T(8,128)(2,1)}, bf16[4,32,512]{2,1,0:T(8,128)(2,1)S(1)}, u32[]{:S(2)}, u32[]{:S(2)}) collective-permute-start(bf16[4,32,512]{2,1,0:T(8,128)(2,1)} %get-tuple-element.52), channel_id=1, source_target_pairs={{0,12},{4,0},{8,4},{12,8},{1,13},{5,1},{9,5},{13,9},{2,14},{6,2},{... | collective-permute-start | bytes 393224 | tf_op jit(solution)/shard_map/ppermute | solution.py:546
  63.6 2.8 %collective-permute-start.1 = (bf16[32,4,512]{2,1,0:T(4,128)(2,1)}, bf16[32,4,512]{2,1,0:T(4,128)(2,1)S(1)}, u32[]{:S(2)}, u32[]{:S(2)}) collective-permute-start(bf16[32,4,512]{2,1,0:T(4,128)(2,1)} %get-tuple-element.53), channel_id=1, source_target_pairs={{0,3},{1,0},{2,1},{3,2},{4,7},{5,4},{6,5},{7,6},{8,11},{9,8},{10,9... | collective-permute-start | bytes 393224 | tf_op jit(solution)/shard_map/ppermute | solution.py:547
  67.4 3.8 %collective-permute-done.2.corner_hbm = bf16[4,4,512]{2,1,0:T(4,128)(2,1)S(1)} collective-permute-done((bf16[4,4,512]{2,1,0:T(4,128)(2,1)}, bf16[4,4,512]{2,1,0:T(4,128)(2,1)S(1)}, u32[]{:S(2)}, u32[]{:S(2)}) %collective-permute-start.2) | collective-permute-done | bytes 16416 | tf_op jit(solution)/shard_map/ppermute | solution.py:551
  72.6 28.4 %block.1 = (f32[5,4,8,2,8,128]{5,4,3,2,1,0:T(8,128)}, f32[4,4,8,2,8,128]{5,4,3,2,1,0:T(8,128)}, f32[5,4,8,2,8,128]{5,4,3,2,1,0:T(8,128)}, f32[4,4,8,2,8,128]{5,4...) custom-call(s32[2]{0:T(128)} %pad_add_fusion.flag_ref, ...), custom_call_target="tpu_custom_call" | custom-call | flops 16000000000 | bytes 25165824 | tf_op jit(solution)/shard_map/block/pallas_call | solution.py:389
  101.6 3.6 %output.2._ = f32[32,32,512]{2,1,0:T(8,128)} custom-call(bf16[1024,512]{1,0:T(8,128)(2,1)} %get-tuple-element.66.x_ref.refs_0_, bf16[512,1024]{1,0:T(8,128)(2,1)} %get-tuple-element.67.ahi_ref.refs_1_, bf16[512,1024]{1,0:T(8,128)(2,1)} %get-tuple-element.68.alo_ref.refs_2_, bf16[512,512]{1,0:T(8,128)(2,1)} %copy-done.1, bf16[512,512]{1,0:T(8,128)(2,1)} %copy-done), custom_call_target="tpu_custom_call" | custom-call | flops 800000000 | bytes 5242880 | tf_op jit(solution)/shard_map/output/pallas_call | solution.py:435
  107.4 2.2 %collective-permute-start.12 = (f32[4,4,4,8,128]{4,3,2,1,0:T(8,128)S(1)}, f32[4,4,4,8,128]{4,3,2,1,0:T(8,128)S(1)}, u32[]{:S(2)}, u32[]{:S(2)}) collective-permute-start(f32[4,4,4,8,128]{4,3,2,1,0:T(8,128)S(1)} %get-tuple-element.92), channel_id=1, source_target_pairs={{0,4},{4,8},{8,12},{12,0},{1,5},{5,9},{9,13},{13,1},{2,6},{6,10},{... | collective-permute-start | bytes 786440 | tf_op jit(solution)/shard_map/ppermute | solution.py:556
  110.6 3.7 %output.3 = f32[32,32,512]{2,1,0:T(8,128)} custom-call(f32[32,32,512]{2,1,0:T(8,128)} %output.2._, bf16[1024,512]{1,0:T(8,128)(2,1)} %get-tuple-element.66.x_ref.refs_0_, bf16[512,1024]{1,0:T(8,128)(2,1)} %get-tuple-element.67.ahi_ref.refs_1_, bf16[512,1024]{1,0:T(8,128)(2,1)} %get-tuple-element.68.alo_ref.refs_2_, ...), custom_call_target="tpu_custom_call", output_to_operand_aliasing={{}: (0, {})} | custom-call | flops 800000000 | bytes 5242880 | tf_op jit(solution)/shard_map/output/pallas_call | solution.py:435
  114.6 1.9 %collective-permute-start.4 = (f32[5,4,4,8,128]{4,3,2,1,0:T(8,128)S(1)}, f32[5,4,4,8,128]{4,3,2,1,0:T(8,128)S(1)}, u32[]{:S(2)}, u32[]{:S(2)}) collective-permute-start(f32[5,4,4,8,128]{4,3,2,1,0:T(8,128)S(1)} %get-tuple-element.89), channel_id=1, source_target_pairs={{0,2},{1,3},{2,0},{3,1},{4,6},{5,7},{6,4},{7,5},{8,10},{9,11},{10,... | collective-permute-start | bytes 983048 | tf_op jit(solution)/shard_map/ppermute | solution.py:556
  116.5 1.8 %collective-permute-start.5 = (f32[5,4,4,8,128]{4,3,2,1,0:T(8,128)S(1)}, f32[5,4,4,8,128]{4,3,2,1,0:T(8,128)S(1)}, u32[]{:S(2)}, u32[]{:S(2)}) collective-permute-start(f32[5,4,4,8,128]{4,3,2,1,0:T(8,128)S(1)} %get-tuple-element.88), channel_id=1, source_target_pairs={{0,1},{1,2},{2,3},{3,0},{4,5},{5,6},{6,7},{7,4},{8,9},{9,10},{10,1... | collective-permute-start | bytes 983048 | tf_op jit(solution)/shard_map/ppermute | solution.py:556
  118.3 1.4 collective-permute-start.6
  119.8 2.5 %collective-permute-done.12 = f32[4,4,4,8,128]{4,3,2,1,0:T(8,128)S(1)} collective-permute-done((f32[4,4,4,8,128]{4,3,2,1,0:T(8,128)S(1)}, f32[4,4,4,8,128]{4,3,2,1,0:T(8,128)S(1)}, u32[]{:S(2)}, u32[]{:S(2)}) %collective-permute-start.12) | collective-permute-done | bytes 262176 | tf_op jit(solution)/shard_map/ppermute | solution.py:556
  124.5 2.0 %collective-permute-start.15 = (f32[4,4,8,128]{3,2,1,0:T(8,128)S(1)}, f32[4,4,8,128]{3,2,1,0:T(8,128)S(1)}, u32[]{:S(2)}, u32[]{:S(2)}) collective-permute-start(f32[4,4,8,128]{3,2,1,0:T(8,128)S(1)} %get-tuple-element.100), channel_id=1, source_target_pairs={{0,1},{1,2},{2,3},{3,0},{4,5},{5,6},{6,7},{7,4},{8,9},{9,10},{10,1... | collective-permute-start | bytes 196616 | tf_op jit(solution)/shard_map/ppermute | solution.py:556
  126.9 2.7 %collective-permute-start.16 = (f32[4,4,8,128]{3,2,1,0:T(8,128)S(1)}, f32[4,4,8,128]{3,2,1,0:T(8,128)S(1)}, u32[]{:S(2)}, u32[]{:S(2)}) collective-permute-start(f32[4,4,8,128]{3,2,1,0:T(8,128)S(1)} %get-tuple-element.99), channel_id=1, source_target_pairs={{0,3},{1,0},{2,1},{3,2},{4,7},{5,4},{6,5},{7,6},{8,11},{9,8},{10,9... | collective-permute-start | bytes 196616 | tf_op jit(solution)/shard_map/ppermute | solution.py:556
  129.6 3.3 %collective-permute-done.5 = f32[5,4,4,8,128]{4,3,2,1,0:T(8,128)S(1)} collective-permute-done((f32[5,4,4,8,128]{4,3,2,1,0:T(8,128)S(1)}, f32[5,4,4,8,128]{4,3,2,1,0:T(8,128)S(1)}, u32[]{:S(2)}, u32[]{:S(2)}) %collective-permute-start.5) | collective-permute-done | bytes 327712 | tf_op jit(solution)/shard_map/ppermute | solution.py:556
  134.2 2.5 %collective-permute-start.8 = (f32[5,4,8,128]{3,2,1,0:T(8,128)S(1)}, f32[5,4,8,128]{3,2,1,0:T(8,128)S(1)}, u32[]{:S(2)}, u32[]{:S(2)}) collective-permute-start(f32[5,4,8,128]{3,2,1,0:T(8,128)S(1)} %get-tuple-element.98), channel_id=1, source_target_pairs={{0,8},{4,12},{8,0},{12,4},{1,9},{5,13},{9,1},{13,5},{2,10},{6,14},... | collective-permute-start | bytes 245768 | tf_op jit(solution)/shard_map/ppermute | solution.py:556
  136.7 1.6 %collective-permute-done.10 = f32[5,4,8,128]{3,2,1,0:T(8,128)S(1)} collective-permute-done((f32[5,4,8,128]{3,2,1,0:T(8,128)S(1)}, f32[5,4,8,128]{3,2,1,0:T(8,128)S(1)}, u32[]{:S(2)}, u32[]{:S(2)}) %collective-permute-start.10) | collective-permute-done | bytes 81952 | tf_op jit(solution)/shard_map/ppermute | solution.py:556
  138.3 2.6 %collective-permute-done.8 = f32[5,4,8,128]{3,2,1,0:T(8,128)S(1)} collective-permute-done((f32[5,4,8,128]{3,2,1,0:T(8,128)S(1)}, f32[5,4,8,128]{3,2,1,0:T(8,128)S(1)}, u32[]{:S(2)}, u32[]{:S(2)}) %collective-permute-start.8) | collective-permute-done | bytes 81952 | tf_op jit(solution)/shard_map/ppermute | solution.py:556
  143.5 1.5 collective-permute-start.18
  145.0 1.8 %collective-permute-start.19 = (f32[9,8,128]{2,1,0:T(8,128)S(1)}, f32[9,8,128]{2,1,0:T(8,128)S(1)}, u32[]{:S(2)}, u32[]{:S(2)}) collective-permute-start(f32[9,8,128]{2,1,0:T(8,128)S(1)} %get-tuple-element.102), channel_id=1, source_target_pairs={{0,96},{16,112},{32,0},{48,16},{64,32},{80,48},{96,64},{112,80},{1... | collective-permute-start | bytes 110600 | tf_op jit(solution)/shard_map/ppermute | solution.py:556
  146.8 1.7 %collective-permute-done.17 = f32[9,8,128]{2,1,0:T(8,128)S(1)} collective-permute-done((f32[9,8,128]{2,1,0:T(8,128)S(1)}, f32[9,8,128]{2,1,0:T(8,128)S(1)}, u32[]{:S(2)}, u32[]{:S(2)}) %collective-permute-start.17) | collective-permute-done | bytes 36896 | tf_op jit(solution)/shard_map/ppermute | solution.py:556
  149.6 1.5 band.1
  (86 shorter events, 22.1 us)
Async XLA Ops:
  3.7 5.7 %copy-start.19 = (s32[1,1,8]{2,1,0:T(1,128)S(1)}, s32[1,1,8]{2,1,0:T(1,128)}, u32[]{:S(2)}) copy-start(s32[1,1,8]{2,1,0:T(1,128)} %param.10) | copy-start | bytes 100
  3.7 5.7 %copy-start.20 = (s32[1,1,8,1]{2,3,1,0:T(1,128)S(1)}, s32[1,1,8,1]{2,3,1,0:T(1,128)}, u32[]{:S(2)}) copy-start(s32[1,1,8,1]{2,3,1,0:T(1,128)} %param.9) | copy-start | bytes 100
  3.7 6.3 %copy-start.9 = (f32[512,1536]{1,0:T(8,128)S(1)}, f32[512,1536]{1,0:T(8,128)}, u32[]{:S(2)}) copy-start(f32[512,1536]{1,0:T(8,128)} %param.12) | copy-start | bytes 9437188
  3.7 33.0 %all-to-all-start = ((bf16[8,2,128,512]{3,2,1,0:T(8,128)(2,1)}), bf16[8,2,128,512]{3,2,1,0:T(8,128)(2,1)}, u32[]{:S(2)}, u32[]{:S(2)}) async-start(bf16[8,2,128,512]{3,2,1,0:T(8,128)(2,1)} %copy.37), calls=%async_computation | async-start | bytes 4194304 | tf_op jit(solution)/shard_map/all_to_all | solution.py:508
  10.1 4.8 %copy-start.15 = (f32[512]{0:T(512)S(1)}, f32[512]{0:T(512)}, u32[]{:S(2)}) copy-start(f32[512]{0:T(512)} %param.11) | copy-start | bytes 6148
  12.4 4.0 %copy-start.2 = (f32[1,1,32,32,512]{4,3,2,1,0:T(8,128)S(1)}, f32[1,1,32,32,512]{4,3,2,1,0:T(8,128)}, u32[]{:S(2)}) copy-start(f32[1,1,32,32,512]{4,3,2,1,0:T(8,128)} %param.15) | copy-start | bytes 6291460
  16.4 9.2 %copy-start = (bf16[512,512]{1,0:T(8,128)(2,1)}, bf16[512,512]{1,0:T(8,128)(2,1)S(1)}, u32[]{:S(2)}) copy-start(bf16[512,512]{1,0:T(8,128)(2,1)S(1)} %get-tuple-element.70.plo_ref.refs_4_) | copy-start | bytes 1572868
  16.4 9.2 %copy-start.1 = (bf16[512,512]{1,0:T(8,128)(2,1)}, bf16[512,512]{1,0:T(8,128)(2,1)S(1)}, u32[]{:S(2)}) copy-start(bf16[512,512]{1,0:T(8,128)(2,1)S(1)} %get-tuple-element.69.phi_ref.refs_3_) | copy-start | bytes 1572868
  16.4 8.4 %copy-start.8 = (f32[512,1536]{0,1:T(8,128)S(1)}, f32[512,1536]{0,1:T(8,128)}, u32[]{:S(2)}) copy-start(f32[512,1536]{0,1:T(8,128)} %copy.39) | copy-start | bytes 9437188
  24.7 2.8 %copy-start.4 = (bf16[1024,512]{1,0:T(8,128)(2,1)}, bf16[1024,512]{1,0:T(8,128)(2,1)S(1)}, u32[]{:S(2)}) copy-start(bf16[1024,512]{1,0:T(8,128)(2,1)S(1)} %get-tuple-element.58.uhi_hbm) | copy-start | bytes 3145732
  60.6 10.6 %collective-permute-start = (bf16[4,32,512]{2,1,0:T(8,128)(2,1)}, bf16[4,32,512]{2,1,0:T(8,128)(2,1)S(1)}, u32[]{:S(2)}, u32[]{:S(2)}) collective-permute-start(bf16[4,32,512]{2,1,0:T(8,128)(2,1)} %get-tuple-element.52), channel_id=1, source_target_pairs={{0,12},{4,0},{8,4},{12,8},{1,13},{5,1},{9,5},{13,9},{2,14},{6,2},{... | collective-permute-start | bytes 393224 | tf_op jit(solution)/shard_map/ppermute | solution.py:546
  63.6 7.6 %collective-permute-start.1 = (bf16[32,4,512]{2,1,0:T(4,128)(2,1)}, bf16[32,4,512]{2,1,0:T(4,128)(2,1)S(1)}, u32[]{:S(2)}, u32[]{:S(2)}) collective-permute-start(bf16[32,4,512]{2,1,0:T(4,128)(2,1)} %get-tuple-element.53), channel_id=1, source_target_pairs={{0,3},{1,0},{2,1},{3,2},{4,7},{5,4},{6,5},{7,6},{8,11},{9,8},{10,9... | collective-permute-start | bytes 393224 | tf_op jit(solution)/shard_map/ppermute | solution.py:547
  66.4 4.8 %collective-permute-start.2 = (bf16[4,4,512]{2,1,0:T(4,128)(2,1)}, bf16[4,4,512]{2,1,0:T(4,128)(2,1)S(1)}, u32[]{:S(2)}, u32[]{:S(2)}) collective-permute-start(bf16[4,4,512]{2,1,0:T(4,128)(2,1)} %get-tuple-element.54), channel_id=1, source_target_pairs={{0,15},{1,12},{2,13},{3,14},{4,3},{5,0},{6,1},{7,2},{8,7},{9,4},{1... | collective-permute-start | bytes 49160 | tf_op jit(solution)/shard_map/ppermute | solution.py:551
  101.0 13.3 %collective-permute-start.3 = (f32[5,4,8,2,8,128]{5,4,3,2,1,0:T(8,128)}, f32[5,4,8,2,8,128]{5,4,3,2,1,0:T(8,128)S(1)}, u32[]{:S(2)}, u32[]{:S(2)}) collective-permute-start(f32[5,4,8,2,8,128]{5,4,3,2,1,0:T(8,128)} %get-tuple-element.64), channel_id=1, source_target_pairs={{0,16},{16,0},{32,48},{48,32},{64,80},{80,64},{96,112},{112,96},{1... | collective-permute-start | bytes 3932168 | tf_op jit(solution)/shard_map/ppermute | solution.py:572
  101.1 4.7 %collective-permute-start.7 = (f32[4,4,8,2,8,128]{5,4,3,2,1,0:T(8,128)}, f32[4,4,8,2,8,128]{5,4,3,2,1,0:T(8,128)S(1)}, u32[]{:S(2)}, u32[]{:S(2)}) collective-permute-start(f32[4,4,8,2,8,128]{5,4,3,2,1,0:T(8,128)} %get-tuple-element.65), channel_id=1, source_target_pairs={{0,16},{16,0},{32,48},{48,32},{64,80},{80,64},{96,112},{112,96},{1... | collective-permute-start | bytes 3145736 | tf_op jit(solution)/shard_map/ppermute | solution.py:573
  101.6 4.2 %copy-start.11 = (f32[4,4,8,2,8,128]{5,4,3,2,1,0:T(8,128)S(1)}, f32[4,4,8,2,8,128]{5,4,3,2,1,0:T(8,128)}, u32[]{:S(2)}) copy-start(f32[4,4,8,2,8,128]{5,4,3,2,1,0:T(8,128)} %get-tuple-element.77) | copy-start | bytes 3145732
  106.7 11.6 %collective-permute-start.11 = (f32[4,4,4,8,128]{4,3,2,1,0:T(8,128)}, f32[4,4,4,8,128]{4,3,2,1,0:T(8,128)S(1)}, u32[]{:S(2)}, u32[]{:S(2)}) collective-permute-start(f32[4,4,4,8,128]{4,3,2,1,0:T(8,128)} %get-tuple-element.93), channel_id=1, source_target_pairs={{0,8},{4,12},{8,0},{12,4},{1,9},{5,13},{9,1},{13,5},{2,10},{6,14},... | collective-permute-start | bytes 786440 | tf_op jit(solution)/shard_map/ppermute | solution.py:556
  107.4 14.9 %collective-permute-start.12 = (f32[4,4,4,8,128]{4,3,2,1,0:T(8,128)S(1)}, f32[4,4,4,8,128]{4,3,2,1,0:T(8,128)S(1)}, u32[]{:S(2)}, u32[]{:S(2)}) collective-permute-start(f32[4,4,4,8,128]{4,3,2,1,0:T(8,128)S(1)} %get-tuple-element.92), channel_id=1, source_target_pairs={{0,4},{4,8},{8,12},{12,0},{1,5},{5,9},{9,13},{13,1},{2,6},{6,10},{... | collective-permute-start | bytes 786440 | tf_op jit(solution)/shard_map/ppermute | solution.py:556
  109.5 12.7 %collective-permute-start.13 = (f32[4,4,4,8,128]{4,3,2,1,0:T(8,128)S(1)}, f32[4,4,4,8,128]{4,3,2,1,0:T(8,128)}, u32[]{:S(2)}, u32[]{:S(2)}) collective-permute-start(f32[4,4,4,8,128]{4,3,2,1,0:T(8,128)S(1)} %get-tuple-element.91), channel_id=1, source_target_pairs={{0,12},{4,0},{8,4},{12,8},{1,13},{5,1},{9,5},{13,9},{2,14},{6,2},{... | collective-permute-start | bytes 786440 | tf_op jit(solution)/shard_map/ppermute | solution.py:556
  110.6 3.7 %copy-start.10 = (f32[5,4,8,2,8,128]{5,4,3,2,1,0:T(8,128)S(1)}, f32[5,4,8,2,8,128]{5,4,3,2,1,0:T(8,128)}, u32[]{:S(2)}) copy-start(f32[5,4,8,2,8,128]{5,4,3,2,1,0:T(8,128)} %get-tuple-element.63) | copy-start | bytes 3932164
  114.6 12.3 %collective-permute-start.4 = (f32[5,4,4,8,128]{4,3,2,1,0:T(8,128)S(1)}, f32[5,4,4,8,128]{4,3,2,1,0:T(8,128)S(1)}, u32[]{:S(2)}, u32[]{:S(2)}) collective-permute-start(f32[5,4,4,8,128]{4,3,2,1,0:T(8,128)S(1)} %get-tuple-element.89), channel_id=1, source_target_pairs={{0,2},{1,3},{2,0},{3,1},{4,6},{5,7},{6,4},{7,5},{8,10},{9,11},{10,... | collective-permute-start | bytes 983048 | tf_op jit(solution)/shard_map/ppermute | solution.py:556
  116.5 16.4 %collective-permute-start.5 = (f32[5,4,4,8,128]{4,3,2,1,0:T(8,128)S(1)}, f32[5,4,4,8,128]{4,3,2,1,0:T(8,128)S(1)}, u32[]{:S(2)}, u32[]{:S(2)}) collective-permute-start(f32[5,4,4,8,128]{4,3,2,1,0:T(8,128)S(1)} %get-tuple-element.88), channel_id=1, source_target_pairs={{0,1},{1,2},{2,3},{3,0},{4,5},{5,6},{6,7},{7,4},{8,9},{9,10},{10,1... | collective-permute-start | bytes 983048 | tf_op jit(solution)/shard_map/ppermute | solution.py:556
  118.3 15.3 %collective-permute-start.6 = (f32[5,4,4,8,128]{4,3,2,1,0:T(8,128)S(1)}, f32[5,4,4,8,128]{4,3,2,1,0:T(8,128)S(1)}, u32[]{:S(2)}, u32[]{:S(2)}) collective-permute-start(f32[5,4,4,8,128]{4,3,2,1,0:T(8,128)S(1)} %get-tuple-element.87), channel_id=1, source_target_pairs={{0,3},{1,0},{2,1},{3,2},{4,7},{5,4},{6,5},{7,6},{8,11},{9,8},{10,9... | collective-permute-start | bytes 983048 | tf_op jit(solution)/shard_map/ppermute | solution.py:556
  123.3 13.3 %collective-permute-start.14 = (f32[4,4,8,128]{3,2,1,0:T(8,128)S(1)}, f32[4,4,8,128]{3,2,1,0:T(8,128)S(1)}, u32[]{:S(2)}, u32[]{:S(2)}) collective-permute-start(f32[4,4,8,128]{3,2,1,0:T(8,128)S(1)} %get-tuple-element.101), channel_id=1, source_target_pairs={{0,2},{1,3},{2,0},{3,1},{4,6},{5,7},{6,4},{7,5},{8,10},{9,11},{10,... | collective-permute-start | bytes 196616 | tf_op jit(solution)/shard_map/ppermute | solution.py:556
  124.5 12.2 %collective-permute-start.15 = (f32[4,4,8,128]{3,2,1,0:T(8,128)S(1)}, f32[4,4,8,128]{3,2,1,0:T(8,128)S(1)}, u32[]{:S(2)}, u32[]{:S(2)}) collective-permute-start(f32[4,4,8,128]{3,2,1,0:T(8,128)S(1)} %get-tuple-element.100), channel_id=1, source_target_pairs={{0,1},{1,2},{2,3},{3,0},{4,5},{5,6},{6,7},{7,4},{8,9},{9,10},{10,1... | collective-permute-start | bytes 196616 | tf_op jit(solution)/shard_map/ppermute | solution.py:556
  126.9 9.8 %collective-permute-start.16 = (f32[4,4,8,128]{3,2,1,0:T(8,128)S(1)}, f32[4,4,8,128]{3,2,1,0:T(8,128)S(1)}, u32[]{:S(2)}, u32[]{:S(2)}) collective-permute-start(f32[4,4,8,128]{3,2,1,0:T(8,128)S(1)} %get-tuple-element.99), channel_id=1, source_target_pairs={{0,3},{1,0},{2,1},{3,2},{4,7},{5,4},{6,5},{7,6},{8,11},{9,8},{10,9... | collective-permute-start | bytes 196616 | tf_op jit(solution)/shard_map/ppermute | solution.py:556
  133.8 4.5 %collective-permute-start.10 = (f32[5,4,8,128]{3,2,1,0:T(8,128)S(1)}, f32[5,4,8,128]{3,2,1,0:T(8,128)S(1)}, u32[]{:S(2)}, u32[]{:S(2)}) collective-permute-start(f32[5,4,8,128]{3,2,1,0:T(8,128)S(1)} %get-tuple-element.96), channel_id=1, source_target_pairs={{0,12},{4,0},{8,4},{12,8},{1,13},{5,1},{9,5},{13,9},{2,14},{6,2},{... | collective-permute-start | bytes 245768 | tf_op jit(solution)/shard_map/ppermute | solution.py:556
  134.2 6.8 %collective-permute-start.8 = (f32[5,4,8,128]{3,2,1,0:T(8,128)S(1)}, f32[5,4,8,128]{3,2,1,0:T(8,128)S(1)}, u32[]{:S(2)}, u32[]{:S(2)}) collective-permute-start(f32[5,4,8,128]{3,2,1,0:T(8,128)S(1)} %get-tuple-element.98), channel_id=1, source_target_pairs={{0,8},{4,12},{8,0},{12,4},{1,9},{5,13},{9,1},{13,5},{2,10},{6,14},... | collective-permute-start | bytes 245768 | tf_op jit(solution)/shard_map/ppermute | solution.py:556
  136.7 5.7 %collective-permute-start.9 = (f32[5,4,8,128]{3,2,1,0:T(8,128)S(1)}, f32[5,4,8,128]{3,2,1,0:T(8,128)S(1)}, u32[]{:S(2)}, u32[]{:S(2)}) collective-permute-start(f32[5,4,8,128]{3,2,1,0:T(8,128)S(1)} %get-tuple-element.97), channel_id=1, source_target_pairs={{0,4},{4,8},{8,12},{12,0},{1,5},{5,9},{9,13},{13,1},{2,6},{6,10},{... | collective-permute-start | bytes 245768 | tf_op jit(solution)/shard_map/ppermute | solution.py:556
  143.0 5.5 %collective-permute-start.17 = (f32[9,8,128]{2,1,0:T(8,128)S(1)}, f32[9,8,128]{2,1,0:T(8,128)S(1)}, u32[]{:S(2)}, u32[]{:S(2)}) collective-permute-start(f32[9,8,128]{2,1,0:T(8,128)S(1)} %get-tuple-element.104), channel_id=1, source_target_pairs={{0,64},{16,80},{32,96},{48,112},{64,0},{80,16},{96,32},{112,48},{1... | collective-permute-start | bytes 110600 | tf_op jit(solution)/shard_map/ppermute | solution.py:556
  143.5 5.3 %collective-permute-start.18 = (f32[9,8,128]{2,1,0:T(8,128)S(1)}, f32[9,8,128]{2,1,0:T(8,128)S(1)}, u32[]{:S(2)}, u32[]{:S(2)}) collective-permute-start(f32[9,8,128]{2,1,0:T(8,128)S(1)} %get-tuple-element.105), channel_id=1, source_target_pairs={{0,32},{16,48},{32,64},{48,80},{64,96},{80,112},{96,0},{112,16},{1... | collective-permute-start | bytes 110600 | tf_op jit(solution)/shard_map/ppermute | solution.py:556
  145.0 4.0 %collective-permute-start.19 = (f32[9,8,128]{2,1,0:T(8,128)S(1)}, f32[9,8,128]{2,1,0:T(8,128)S(1)}, u32[]{:S(2)}, u32[]{:S(2)}) collective-permute-start(f32[9,8,128]{2,1,0:T(8,128)S(1)} %get-tuple-element.102), channel_id=1, source_target_pairs={{0,96},{16,112},{32,0},{48,16},{64,32},{80,48},{96,64},{112,80},{1... | collective-permute-start | bytes 110600 | tf_op jit(solution)/shard_map/ppermute | solution.py:556
  (10 other events, 8.1 us)
